TPU v7x, 128 devices: a whole 4x4x4 slice. The times are simulated.
128 devices in a mesh: lat: 8 (over x_hi, y), lon: 8 (over z, core), mp: 2 (over x_lo).
Axes of the slice: x: 4 (x_hi: 2, x_lo: 2; x = x_hi * 2 + x_lo), y: 4, z: 4, core: 2. Of those that a mesh axis runs over, the one named last changes fastest.
Arguments:
- fields: bfloat16 [256, 256, 512], P('lat', 'lon', 'mp'), may hold values from -6 to 6
- qkv_plain: bfloat16 [512, 3, 512], P(None, None, 'mp'), may hold values from -0.25 to 0.25
- out_plain: bfloat16 [512, 512], P('mp'), may hold values from -0.25 to 0.25
- qkv_shift: bfloat16 [512, 3, 512], P(None, None, 'mp'), may hold values from -0.25 to 0.25
- out_shift: bfloat16 [512, 512], P('mp'), may hold values from -0.25 to 0.25
- cotangent: bfloat16 [256, 256, 512], P('lat', 'lon', 'mp'), may hold values from -6 to 6
Outputs:
- result: bfloat16 [256, 256, 512], P('lat', 'lon', 'mp')
- grad_fields: bfloat16 [256, 256, 512], P('lat', 'lon', 'mp')
- grad_qkv_plain: float32 [512, 3, 512], P(None, None, 'mp')
- grad_out_plain: float32 [512, 512], P('mp')
- grad_qkv_shift: float32 [512, 3, 512], P(None, None, 'mp')
- grad_out_shift: float32 [512, 512], P('mp')
All inputs are finite; a program needn't handle non-finite values.
Results may differ from a plain program's by a relative error of at most 0.034.
Values may be sent and summed in bfloat16 or wider, within the bound.
A program may use at most 128 MiB of HBM per device.

v0:
```python
import jax
import jax.numpy as jnp
from jax import lax
from jax.sharding import PartitionSpec as P

HEAD_DIM = 32
WL = 8
WO = 16


def padded_2(block, sides, width, periodic):
    for axis, dim in sides:
        count = lax.axis_size(axis)
        forward = [(i, i + 1) for i in range(count - 1)]
        if periodic:
            forward.append((count - 1, 0))
        backward = [(target, source) for source, target in forward]
        low = lax.ppermute(
            lax.slice_in_dim(block, block.shape[dim] - width, None, axis=dim), axis, forward
        )
        high = lax.ppermute(lax.slice_in_dim(block, 0, width, axis=dim), axis, backward)
        block = jnp.concatenate([low, block, high], axis=dim)
    return block


def to_windows(token_grid):
    grid_rows, grid_cols = (token_grid.shape[0], token_grid.shape[1])
    trailing = token_grid.shape[2:]
    blocked = token_grid.reshape((grid_rows // WL, WL, grid_cols // WO, WO) + trailing)
    perm_order = (0, 2, 1, 3) + tuple(range(4, 4 + len(trailing)))
    return blocked.transpose(perm_order).reshape(
        (grid_rows // WL * (grid_cols // WO), WL * WO) + trailing
    )


def from_windows(windowed, grid_rows, grid_cols):
    trailing = windowed.shape[2:]
    blocked = windowed.reshape((grid_rows // WL, grid_cols // WO, WL, WO) + trailing)
    perm_order = (0, 2, 1, 3) + tuple(range(4, 4 + len(trailing)))
    return blocked.transpose(perm_order).reshape((grid_rows, grid_cols) + trailing)


def normalize(token_grid):
    average = jnp.mean(token_grid, -1, keepdims=True)
    centred = token_grid - average
    inv_scale = lax.rsqrt(jnp.mean(centred * centred, -1, keepdims=True) + 1e-05)
    return (centred * inv_scale, inv_scale)


def norm_back(standard, inv_scale, gradient):
    return inv_scale * (
        gradient
        - jnp.mean(gradient, -1, keepdims=True)
        - standard * jnp.mean(gradient * standard, -1, keepdims=True)
    )


def attention_core(projected, band_windows):
    windows, win_size = (projected.shape[0], projected.shape[1])
    head_count = projected.shape[3] // HEAD_DIM
    blocked = projected.reshape(windows, win_size, 3, head_count, HEAD_DIM)
    queries, key_part, values = (blocked[:, :, 0], blocked[:, :, 1], blocked[:, :, 2])
    scores = jnp.einsum(
        "wqhe,wkhe->whqk", queries, key_part, preferred_element_type=jnp.float32
    ) * HEAD_DIM ** (-0.5)
    same_band = (band_windows[:, :, None] == band_windows[:, None, :])[:, None]
    raised = jnp.where(same_band, jnp.exp(scores), 0.0)
    softmax = (raised / jnp.sum(raised, -1, keepdims=True)).astype(jnp.bfloat16)
    mixture = jnp.einsum(
        "whqk,wkhe->wqhe", softmax, values, preferred_element_type=jnp.float32
    ).astype(jnp.bfloat16)
    return mixture.reshape(windows, win_size, head_count * HEAD_DIM)


def group_forward(normed, band_windows, qkv_weight, out_weight):
    projected = jnp.einsum(
        "wtd,dce->wtce", normed, qkv_weight, preferred_element_type=jnp.float32
    ).astype(jnp.bfloat16)
    mixture, core_back = jax.vjp(
        lambda projected_in: attention_core(projected_in, band_windows), projected
    )
    partial_value = jnp.einsum(
        "wte,ed->wtd", mixture, out_weight, preferred_element_type=jnp.float32
    )
    return (partial_value, (mixture, core_back))


def group_backward(normed, stored, qkv_weight, out_weight, gradient):
    mixture, core_back = stored
    grad_out = jnp.einsum("wte,wtd->ed", mixture, gradient, preferred_element_type=jnp.float32)
    grad_mixture = jnp.einsum(
        "wtd,ed->wte", gradient, out_weight, preferred_element_type=jnp.float32
    ).astype(jnp.bfloat16)
    grad_projected = core_back(grad_mixture)[0]
    grad_qkv = jnp.einsum(
        "wtd,wtce->dce", normed, grad_projected, preferred_element_type=jnp.float32
    )
    grad_normed = jnp.einsum(
        "wtce,dce->wtd", grad_projected, qkv_weight, preferred_element_type=jnp.float32
    )
    return (grad_normed, grad_qkv, grad_out)


def block_forward(token_grid, band_grid, groups):
    grid_rows, grid_cols = (token_grid.shape[0], token_grid.shape[1])
    standard, inv_scale = normalize(token_grid)
    normed = to_windows(standard.astype(jnp.bfloat16))
    band_windows = to_windows(band_grid)
    partials, stored_list = ([], [])
    for qkv_weight, out_weight in groups:
        partial_value, stored = group_forward(normed, band_windows, qkv_weight, out_weight)
        partials.append(from_windows(partial_value, grid_rows, grid_cols))
        stored_list.append(stored)
    return (partials, (standard, inv_scale, normed, stored_list))


def block_backward(stored_block, groups, grad_grid):
    standard, inv_scale, normed, stored_list = stored_block
    grid_rows, grid_cols = (standard.shape[0], standard.shape[1])
    grad_windows = to_windows(grad_grid)
    contributions, qkv_list, out_list = ([], [], [])
    for stored, (qkv_weight, out_weight) in zip(stored_list, groups):
        grad_normed, grad_qkv, grad_out = group_backward(
            normed, stored, qkv_weight, out_weight, grad_windows
        )
        contributions.append(
            norm_back(standard, inv_scale, from_windows(grad_normed, grid_rows, grid_cols))
        )
        qkv_list.append(grad_qkv)
        out_list.append(grad_out)
    return (contributions, qkv_list, out_list)


def fold(gradient, axis_dim, half_width, sender):
    extent_all = gradient.shape[axis_dim]
    lead_rim = lax.slice_in_dim(gradient, 0, half_width, axis=axis_dim)
    tail_rim = lax.slice_in_dim(gradient, extent_all - half_width, extent_all, axis=axis_dim)
    received = sender(jnp.concatenate([lead_rim, tail_rim], axis_dim))
    interior = lax.slice_in_dim(gradient, half_width, extent_all - half_width, axis=axis_dim)
    extent = interior.shape[axis_dim]
    near_part = lax.slice_in_dim(interior, 0, half_width, axis=axis_dim) + lax.slice_in_dim(
        received, 0, half_width, axis=axis_dim
    )
    middle = lax.slice_in_dim(interior, half_width, extent - half_width, axis=axis_dim)
    far_part = lax.slice_in_dim(
        interior, extent - half_width, extent, axis=axis_dim
    ) + lax.slice_in_dim(received, 3 * half_width, 4 * half_width, axis=axis_dim)
    return jnp.concatenate([near_part, middle, far_part], axis_dim)


def assemble(shard):
    return lax.all_gather(shard, "mp", axis=2, tiled=True)


def reduce_heads(term):
    return lax.psum_scatter(
        term.astype(jnp.bfloat16), "mp", scatter_dimension=2, tiled=True
    ).astype(jnp.float32)


def lat_rim(grid_part):
    return padded_2(grid_part, (("lat", 0),), WL // 2, False)


def lat_fold(gradient):
    return fold(
        gradient,
        0,
        WL // 2,
        lambda edge_rims: padded_2(
            edge_rims.astype(jnp.bfloat16), (("lat", 0),), WL // 2, False
        ).astype(edge_rims.dtype),
    )


def row_marks(lat_rows):
    total_rows = lat_rows * lax.axis_size("lat")
    global_rows = (
        lax.axis_index("lat") * lat_rows + jnp.arange(lat_rows + WL, dtype=jnp.int32) - WL // 2
    )
    return ((global_rows >= 0) & (global_rows < total_rows)).astype(jnp.int32)


def on_device(fields, qkv_plain, out_plain, qkv_shift, out_shift, cotangent):
    lat_rows = fields.shape[0]
    half_lat, half_lon = (WL // 2, WO // 2)
    tokens_all = lat_rows * lax.axis_size("lat") * fields.shape[1] * lax.axis_size("lon")
    factor = lax.rsqrt(jnp.float32(tokens_all))
    wide_marks = row_marks(lat_rows)
    lon_cols = fields.shape[1]
    plain_groups = [(qkv_plain, out_plain)]
    shift_groups = [(qkv_shift, out_shift)]
    plain_bands = jnp.ones((lat_rows, lon_cols), jnp.int32)
    shift_bands = jnp.broadcast_to(wide_marks[:, None], (lat_rows + WL, lon_cols + WO))
    partials_plain, stored_plain = block_forward(
        assemble(fields).astype(jnp.float32), plain_bands, plain_groups
    )
    hidden = (fields.astype(jnp.float32) + reduce_heads(partials_plain[0])).astype(jnp.bfloat16)
    widened = padded_2(lat_rim(assemble(hidden)), (("lon", 1),), half_lon, True)
    partials_shift, stored_shift = block_forward(
        widened.astype(jnp.float32), shift_bands, shift_groups
    )
    cropped = partials_shift[0][half_lat : half_lat + lat_rows, half_lon : half_lon + lon_cols]
    result = (hidden.astype(jnp.float32) + reduce_heads(cropped)).astype(jnp.bfloat16)
    padded = jnp.pad(assemble(cotangent), ((half_lat, half_lat), (half_lon, half_lon), (0, 0)))
    contributions, qkv_list_shift, out_list_shift = block_backward(
        stored_shift, shift_groups, padded
    )
    spread = fold(
        reduce_heads(contributions[0]),
        1,
        half_lon,
        lambda edge_rims: padded_2(
            edge_rims.astype(jnp.bfloat16), (("lon", 1),), half_lon, True
        ).astype(edge_rims.dtype),
    )
    grad_hidden = (cotangent.astype(jnp.float32) + lat_fold(spread)).astype(jnp.bfloat16)
    contributions, qkv_list_plain, out_list_plain = block_backward(
        stored_plain, plain_groups, assemble(grad_hidden)
    )
    grad_fields = (grad_hidden.astype(jnp.float32) + reduce_heads(contributions[0])).astype(
        jnp.bfloat16
    )
    gradients = (qkv_list_plain[0], out_list_plain[0], qkv_list_shift[0], out_list_shift[0])
    gradients = lax.psum((gradients[0], gradients[1], gradients[2], gradients[3]), ("lat", "lon"))
    return (
        result,
        grad_fields,
        gradients[0] * factor,
        gradients[1] * factor,
        gradients[2] * factor,
        gradients[3] * factor,
    )


def solution(mesh):
    in_specs = (
        P("lat", "lon", "mp"),
        P(None, None, "mp"),
        P("mp", None),
        P(None, None, "mp"),
        P("mp", None),
        P("lat", "lon", "mp"),
    )
    out_specs = (
        P("lat", "lon", "mp"),
        P("lat", "lon", "mp"),
        P(None, None, "mp"),
        P("mp", None),
        P(None, None, "mp"),
        P("mp", None),
    )
    return jax.shard_map(
        on_device, mesh=mesh, in_specs=in_specs, out_specs=out_specs, check_vma=False
    )
```

profile of v0, /device:TPU:1, one launch (start us, length us, event | category | flops | bytes accessed | tf_op | source)
XLA Modules:
  0.0 1027.5 jit_solution(3378386076637618138)
XLA Ops:
  8.0 28.7 %all-gather.5.cloned.1.call-done = bf16[32,32,512]{2,1,0:T(8,128)(2,1)} async-done(((bf16[32,32,256]{2,1,0:T(8,128)(2,1)}), bf16[32,32,512]{2,1,0:T(8,128)(2,1)}) %all-gather.5.cloned.1.call-update) | async-done | bytes 1048592 | tf_op jit(solution)/shard_map/all_gather | solution.py:152
  56.9 23.9 %reduce-scatter.5.cloned.1.call-done = bf16[32,32,256]{2,1,0:T(8,128)(2,1)} async-done(((bf16[32,32,512]{2,1,0:T(8,128)(2,1)}), bf16[32,32,256]{2,1,0:T(8,128)(2,1)}) %reduce-scatter.5.cloned.1.call-update) | async-done | bytes 524304 | tf_op jit(solution)/shard_map/reduce_scatter | solution.py:156
  83.5 24.4 %all-gather.7.cloned.1.call-done = bf16[32,32,512]{2,1,0:T(8,128)(2,1)} async-done(((bf16[32,32,256]{2,1,0:T(8,128)(2,1)}), bf16[32,32,512]{2,1,0:T(8,128)(2,1)}) %all-gather.7.cloned.1.call-update) | async-done | bytes 1048592 | tf_op jit(solution)/shard_map/all_gather | solution.py:152
  123.0 11.3 %all-gather.9.cloned.1.call-done = bf16[32,32,512]{2,1,0:T(8,128)(2,1)} async-done(((bf16[32,32,256]{2,1,0:T(8,128)(2,1)}), bf16[32,32,512]{2,1,0:T(8,128)(2,1)}) %all-gather.9.cloned.1.call-update) | async-done | bytes 1048592 | tf_op jit(solution)/shard_map/all_gather | solution.py:152
  149.8 4.6 copy.220
  154.4 6.7 fusion.7
  161.1 7.1 fusion.5
  168.2 8.6 fusion.29
  176.8 7.1 fusion.28
  188.0 11.6 %copy.177 = bf16[15,128,3,8,32]{4,3,1,2,0:T(8,128)(2,1)} copy(bf16[15,128,3,8,32]{1,4,3,0,2:T(8,128)(2,1)} %pad_add_fusion) | data formatting | bytes 5898240 | tf_op jit(solution)/shard_map/transpose(jvp())/add_any | solution.py:62
  199.5 14.6 %dot_general.95 = bf16[5,3,8,16,3,256]{5,3,2,4,1,0:T(8,128)(2,1)} reshape(bf16[15,128,3,8,32]{4,3,1,2,0:T(8,128)(2,1)} %copy.177) | data formatting | bytes 5898240 | tf_op jit(solution)/shard_map/wtce,dce->wtd/dot_general | solution.py:98
  214.2 6.8 fusion.54
  227.1 33.8 %reduce-scatter.9.cloned.1.call-done = bf16[40,48,256]{2,1,0:T(8,128)(2,1)} async-done(((bf16[40,48,512]{2,1,0:T(8,128)(2,1)}), bf16[40,48,256]{2,1,0:T(8,128)(2,1)}) %reduce-scatter.9.cloned.1.call-update) | async-done | bytes 983056 | tf_op jit(solution)/shard_map/reduce_scatter | solution.py:156
  278.0 3.5 convolution_convert_fusion.9
  281.6 3.6 copy.170
  285.2 5.1 dot_general.88
  292.3 13.0 %all-gather.11.cloned.1.call-done = bf16[32,32,512]{2,1,0:T(8,128)(2,1)} async-done(((bf16[32,32,256]{2,1,0:T(8,128)(2,1)}), bf16[32,32,512]{2,1,0:T(8,128)(2,1)}) %all-gather.11.cloned.1.call-update) | async-done | bytes 1048592 | tf_op jit(solution)/shard_map/all_gather | solution.py:152
  309.9 3.7 fusion.12
  316.5 4.9 copy.187
  321.4 8.5 dot_general.102
  329.9 3.8 fusion.59
  341.5 5.6 convolution_bitcast_fusion.2
  353.6 8.2 reduce-scatter.11.cloned.1.call-done
  363.8 651.2 %all-reduce.10.cloned.1.call-done = (f32[512,3,256]{2,0,1:T(8,128)}, f32[256,512]{1,0:T(8,128)}, f32[512,3,256]{2,0,1:T(8,128)}, f32[256,512]{1,0:T(8,128)}) async-done(((f32[512,3,256]{2,0,1:T(8,128)}, f32[256,512]{1,0:T(8,128)}, f32[512,3,256]{2,0,1:T(8,128)}, f32[256,512]{1,0:T(8,128)}), (f32[512,3,256]{2,0,1:T(8,128)}, f32[256,512]{1,0:T(8,128)}, f32[512,3,256]{2,0,1:T(8,128)}, ...) | async-done | bytes 4194320 | tf_op jit(solution)/shard_map/psum | solution.py:225
  (192 shorter events, 112.5 us)
Async XLA Ops:
  7.2 139.3 %copy-start = (bf16[512,3,256]{2,0,1:T(8,128)(2,1)S(1)}, bf16[512,3,256]{2,0,1:T(8,128)(2,1)}, u32[]{:S(2)}) copy-start(bf16[512,3,256]{2,0,1:T(8,128)(2,1)} %param.9) | copy-start | bytes 2359300
  7.2 29.5 %all-gather.5.cloned.1.call-start = ((), (), s32[]{:S(2)}) async-start(), calls=%async_computation.4 | async-start | bytes 1572864 | tf_op jit(solution)/shard_map/all_gather | solution.py:152
  7.9 72.9 %reduce-scatter.5.cloned.1.call-start = ((), (), s32[]{:S(2)}) async-start(), calls=%async_computation.5 | async-start | bytes 1572864 | tf_op jit(solution)/shard_map/reduce_scatter | solution.py:156
  54.2 26.6 %copy-start.21 = (bf16[32,32,256]{2,1,0:T(8,128)(2,1)S(1)}, bf16[32,32,256]{2,1,0:T(8,128)(2,1)}, u32[]{:S(2)}) copy-start(bf16[32,32,256]{2,1,0:T(8,128)(2,1)} %param.6) | copy-start | bytes 1572868
  56.9 51.1 %all-gather.7.cloned.1.call-start = ((), (), s32[]{:S(2)}) async-start(), calls=%async_computation.6 | async-start | bytes 1572864 | tf_op jit(solution)/shard_map/all_gather | solution.py:152
  82.9 51.5 %all-gather.9.cloned.1.call-start = ((), (), s32[]{:S(2)}) async-start(), calls=%async_computation.8 | async-start | bytes 1572864 | tf_op jit(solution)/shard_map/all_gather | solution.py:152
  83.4 177.4 %reduce-scatter.9.cloned.1.call-start = ((), (), s32[]{:S(2)}) async-start(), calls=%async_computation.9 | async-start | bytes 2949120 | tf_op jit(solution)/shard_map/reduce_scatter | solution.py:156
  108.9 5.3 collective-permute-start
  112.2 5.7 collective-permute-start.1
  118.7 22.4 %collective-permute-start.2 = (bf16[40,8,512]{2,1,0:T(8,128)(2,1)}, bf16[40,8,512]{2,1,0:T(8,128)(2,1)S(1)}, u32[]{:S(2)}, u32[]{:S(2)}) collective-permute-start(bf16[40,8,512]{2,1,0:T(8,128)(2,1)} %get-tuple-element.18), channel_id=1, source_target_pairs={{0,2},{2,4},{4,6},{6,8},{8,10},{10,12},{12,14},{14,0},{1,3},{3,5},... | collective-permute-start | bytes 983048 | tf_op jit(solution)/shard_map/ppermute | solution.py:18
  122.0 19.2 %collective-permute-start.3 = (bf16[40,8,512]{2,1,0:T(8,128)(2,1)S(1)}, bf16[40,8,512]{2,1,0:T(8,128)(2,1)S(1)}, u32[]{:S(2)}, u32[]{:S(2)}) collective-permute-start(bf16[40,8,512]{2,1,0:T(8,128)(2,1)S(1)} %get-tuple-element.19), channel_id=1, source_target_pairs={{2,0},{4,2},{6,4},{8,6},{10,8},{12,10},{14,12},{0,14},{3,1},{5,3},... | collective-permute-start | bytes 983048 | tf_op jit(solution)/shard_map/ppermute | solution.py:21
  123.0 14.3 %copy-start.25 = (bf16[256,512]{1,0:T(8,128)(2,1)S(1)}, bf16[256,512]{1,0:T(8,128)(2,1)}, u32[]{:S(2)}) copy-start(bf16[256,512]{1,0:T(8,128)(2,1)} %param.10) | copy-start | bytes 786436
  168.2 15.7 %copy-start.7 = (bf16[15,8,128,128]{2,3,1,0:T(8,128)(2,1)}, bf16[15,8,128,128]{2,3,1,0:T(8,128)(2,1)S(1)}, u32[]{:S(2)}) copy-start(bf16[15,8,128,128]{2,3,1,0:T(8,128)(2,1)S(1)} %get-tuple-element.13) | copy-start | bytes 11796484
  226.8 78.5 %all-gather.11.cloned.1.call-start = ((), (), s32[]{:S(2)}) async-start(), calls=%async_computation.10 | async-start | bytes 1572864 | tf_op jit(solution)/shard_map/all_gather | solution.py:152
  261.9 4.3 collective-permute-start.4
  263.7 4.7 collective-permute-start.5
  268.6 4.7 collective-permute-start.6
  271.9 5.0 collective-permute-start.7
  277.9 72.6 %reduce-scatter.7.cloned.1.call-start = ((), (), s32[]{:S(2)}) async-start(), calls=%async_computation.7 | async-start | bytes 1572864 | tf_op jit(solution)/shard_map/reduce_scatter | solution.py:156
  291.2 16.6 %copy-start.26 = (bf16[256,512]{1,0:T(8,128)(2,1)S(1)}, bf16[256,512]{1,0:T(8,128)(2,1)}, u32[]{:S(2)}) copy-start(bf16[256,512]{1,0:T(8,128)(2,1)} %param.8) | copy-start | bytes 786436
  292.3 16.3 %copy-start.6 = (bf16[8,8,128,128]{2,3,1,0:T(8,128)(2,1)S(1)}, bf16[8,8,128,128]{2,3,1,0:T(8,128)(2,1)}, u32[]{:S(2)}) copy-start(bf16[8,8,128,128]{2,3,1,0:T(8,128)(2,1)} %copy-done.5) | copy-start | bytes 6291460
  292.3 69.5 %reduce-scatter.11.cloned.1.call-start = ((), (), s32[]{:S(2)}) async-start(), calls=%async_computation.11 | async-start | bytes 1572864 | tf_op jit(solution)/shard_map/reduce_scatter | solution.py:156
  337.8 677.1 %all-reduce.10.cloned.1.call-start = ((), (), s32[]{:S(2)}) async-start(), calls=%async_computation.12 | async-start | bytes 8388608 | tf_op jit(solution)/shard_map/psum | solution.py:225
  350.5 11.3 %copy-start.16 = (bf16[32,32,256]{2,1,0:T(8,128)(2,1)S(1)}, bf16[32,32,256]{2,1,0:T(8,128)(2,1)}, u32[]{:S(2)}) copy-start(bf16[32,32,256]{2,1,0:T(8,128)(2,1)} %fusion.33) | copy-start | bytes 1572868
  (27 other events, 107.4 us)
Sparse Core Ops, SparseCore 0:
  9.7 26.9 all-gather.4
  57.0 23.7 reduce-scatter.4
  83.1 24.7 all-gather.6
  109.5 24.7 all-gather.8
  227.0 33.8 reduce-scatter.8
  278.1 27.2 all-gather.10
  307.7 23.7 reduce-scatter.6
  337.9 23.7 reduce-scatter.10
  365.1 649.8 all-reduce.9
where the time goes:
time: 1030 us
  waiting for transfers between devices  804 us (78%)
  local copies, waits for them, and re-layouts  85.1 us (8%)
  matrix products  77 us (7%)
  other arithmetic  31.1 us (3%)
  starting transfers between devices  15.4 us (1%)
  between operations  14.8 us (1%)
    psum x1, waiting for transfers between devices, on_device(): lax.psum((gradients[0], gradients[1], gradients[2], gradients[3]), ('lat'...  651 us
    all_gather x4, waiting for transfers between devices, assemble(): return lax.all_gather(shard, 'mp', axis=2, tiled=True)  77.5 us
    reduce_scatter x4, waiting for transfers between devices, reduce_heads(): lax.psum_scatter(term.astype(jnp.bfloat16), 'mp', scatter_dimension=2, ti...  65.9 us
    dot_general x6, matrix products, attention_core(): jnp.einsum('wqhe,wkhe->whqk', queries, key_part, preferred_element_type=j...  25.9 us
    dot_general x2, local copies, waits for them, and re-layouts, group_backward(): jnp.einsum('wtce,dce->wtd', grad_projected, qkv_weight, preferred_element...  23.1 us
  transfers between devices with their start and end apart: 17, of which 12 were waited for; matrix products, arithmetic and copies ran while one was open for 7% of the time, Pallas kernels for 0%

commit v1 on v0

v1 whole, which is shorter than its diff:
```python
import functools

import jax
import jax.numpy as jnp
from jax import lax
from jax.experimental import pallas as pl
from jax.experimental.pallas import tpu as pltpu
from jax.sharding import PartitionSpec as P

BF = jnp.bfloat16
F32 = jnp.float32
MESH = pl.DeviceIdType.MESH
VMEM_LIMIT = 56 * 1024 * 1024
D = 512
HEAD_DIM = 32
SCALE = HEAD_DIM ** -0.5
LOG2E = 1.4426950408889634


def place():
    lat, lon, mp = lax.axis_index("lat"), lax.axis_index("lon"), lax.axis_index("mp")
    return lat, lon, mp


def row_step(lat, mp, step):
    at = lax.rem(lat * 2 + mp + step + 16, 16)
    return at // 2, lax.rem(at, 2)


def barrier(peers):
    sem = pltpu.get_barrier_semaphore()
    for peer in peers:
        pl.semaphore_signal(sem, inc=1, device_id=peer, device_id_type=MESH)
    pl.semaphore_wait(sem, len(peers))


class Sender:
    def __init__(self, send, recv):
        self.send, self.recv, self.used = send, recv, 0

    def __call__(self, src, dst, peer):
        copy = pltpu.make_async_remote_copy(
            src_ref=src,
            dst_ref=dst,
            send_sem=self.send.at[self.used],
            recv_sem=self.recv.at[self.used],
            device_id=peer,
            device_id_type=MESH,
        )
        self.used += 1
        copy.start()
        return copy


def comm_call(kernel, out_shape, sends, collective_id, scratch=(), locals_=1):
    vmem = pl.BlockSpec(memory_space=pltpu.VMEM)

    def call(*args):
        return pl.pallas_call(
            kernel,
            out_shape=out_shape,
            in_specs=[vmem] * len(args),
            out_specs=[vmem] * len(out_shape),
            scratch_shapes=[
                *scratch,
                pltpu.SemaphoreType.DMA((sends,)),
                pltpu.SemaphoreType.DMA((sends,)),
                pltpu.SemaphoreType.DMA((locals_,)),
            ],
            compiler_params=pltpu.CompilerParams(
                collective_id=collective_id,
                has_side_effects=True,
                vmem_limit_bytes=VMEM_LIMIT,
            ),
        )(*args)

    return call


def enter_kernel(
    fc, cc, wqp, wop, wqs, wos, x, c, fqp, fop, fqs, fos, send, recv, local
):
    lat, lon, mp = place()
    near = (lat, lon, 1 - mp)
    far = (lax.rem(lat + 4, 8), lon, 1 - mp)
    core = lax.rem(lon, 2)
    sibling = (lat, lon + 1 - 2 * core, mp)
    barrier([near, far, sibling])
    go = Sender(send, recv)
    lanes = pl.ds(pl.multiple_of(mp * 256, 256), 256)
    other_rows = pl.ds((1 - mp) * 4, 4)
    own_rows = pl.ds(mp * 4, 4)
    first = [go(fc.at[other_rows], x.at[:, :, :, lanes], near)]
    kept = []
    for n, (src, dst) in enumerate(
        (
            (fc.at[own_rows], x.at[:, :, :, lanes]),
            (cc.at[own_rows], c.at[:, :, :, lanes]),
            (wqp, fqp.at[:, :, lanes]),
            (wqs, fqs.at[:, :, lanes]),
            (wop, fop.at[pl.ds(pl.multiple_of(mp * 256, 256), 256)]),
            (wos, fos.at[pl.ds(pl.multiple_of(mp * 256, 256), 256)]),
        )
    ):
        copy = pltpu.make_async_copy(src, dst, local.at[n])
        copy.start()
        kept.append(copy)
    peers = (near, far)
    mine, theirs = [], []
    for src, dst in ((wqp, fqp), (wqs, fqs)):
        for k in range(2):
            rows = pl.ds(pl.multiple_of((k * 2 + core) * 128, 128), 128)
            mine.append((go(src.at[:, rows], dst.at[:, rows, lanes], peers[k]), dst, rows, None))
    for src, dst in ((wop, fop), (wos, fos)):
        for k in range(2):
            rows = pl.ds(pl.multiple_of((k * 2 + core) * 64, 64), 64)
            there = pl.ds(pl.multiple_of(mp * 256 + (k * 2 + core) * 64, 64), 64)
            here = pl.ds(pl.multiple_of((1 - mp) * 256 + (k * 2 + core) * 64, 64), 64)
            mine.append((go(src.at[rows], dst.at[there], peers[k]), dst, None, here))
    first.append(go(cc.at[other_rows], c.at[:, :, :, lanes], near))
    arrived = pl.ds(pl.multiple_of((1 - mp) * 256, 256), 256)
    for copy, dst, rows, here in mine:
        copy.wait_recv()
        spot = dst.at[here] if rows is None else dst.at[:, rows, arrived]
        theirs.append(go(spot, spot, sibling))
    for copy, _, _, _ in mine:
        copy.wait_send()
    for copy in first + theirs:
        copy.wait()
    for copy in kept:
        copy.wait()


def around(lat, lon, mp, step):
    row_lat, row_mp = row_step(lat, mp, step)
    col = lax.rem(lon + step + 8, 8)
    return (row_lat, row_lat * 0 + lon, row_mp), (lat, col, mp), (row_lat, col, row_mp)


def widen_kernel(h, c, hx, cx, send, recv, local):
    lat, lon, mp = place()
    row_prev, col_prev, corner_prev = around(lat, lon, mp, -1)
    row_next, col_next, corner_next = around(lat, lon, mp, 1)
    barrier([row_prev, col_prev, corner_prev, row_next, col_next, corner_next])
    go = Sender(send, recv)
    copies = []
    for src, dst in ((h, hx), (c, cx)):
        copies.append(go(src.at[0], dst.at[4, pl.ds(0, 4)], row_prev))
        copies.append(go(src.at[:, 0], dst.at[pl.ds(0, 4), 4], col_prev))
        copies.append(go(src.at[0, 0], dst.at[4, 4], corner_prev))
    for n, (src, dst) in enumerate(((h, hx), (c, cx))):
        copy = pltpu.make_async_copy(src, dst.at[pl.ds(0, 4), pl.ds(0, 4)], local.at[n])
        copy.start()
        copies.append(copy)
    for copy in copies:
        copy.wait()


def narrow_kernel(a, b, ao, bo, send, recv, local):
    lat, lon, mp = place()
    row_prev, col_prev, corner_prev = around(lat, lon, mp, -1)
    row_next, col_next, corner_next = around(lat, lon, mp, 1)
    barrier([row_prev, col_prev, corner_prev, row_next, col_next, corner_next])
    go = Sender(send, recv)
    copies = []
    low, high = pl.ds(0, 3), pl.ds(1, 3)
    for src, dst in ((a, ao), (b, bo)):
        copies.append(go(src.at[3, low], dst.at[0, high], row_next))
        copies.append(go(src.at[low, 3], dst.at[high, 0], col_next))
        copies.append(go(src.at[3, 3], dst.at[0, 0], corner_next))
    for n, (src, dst) in enumerate(((a, ao), (b, bo))):
        copy = pltpu.make_async_copy(src.at[low, low], dst.at[high, high], local.at[n])
        copy.start()
        copies.append(copy)
    for copy in copies:
        copy.wait()


def leave_kernel(
    r, gf, g, ro, gfo, out, r0, a0, r1, a1, r2, a2, r3, f, send, recv, local
):
    lat, lon, mp = place()
    core, z = lax.rem(lon, 2), lon // 2
    y, x_hi = lax.rem(lat, 4), lat // 4
    near = (lat, lon, 1 - mp)
    far = (lax.rem(lat + 4, 8), lon, 1 - mp)
    opposite = (lax.rem(lat + 4, 8), lon, mp)
    sibling = (lat, lon + 1 - 2 * core, mp)

    def along_y(step):
        return (x_hi * 4 + lax.rem(y + step, 4), lon, mp)

    def along_z(step):
        return (lat, lax.rem(z + step, 4) * 2 + core, mp)

    barrier(
        [near, far, opposite, sibling]
        + [along_y(s) for s in (1, 2, 3)]
        + [along_z(s) for s in (1, 2, 3)]
    )
    go = Sender(send, recv)
    lanes = pl.ds(pl.multiple_of(mp * 256, 256), 256)
    away = pl.ds(pl.multiple_of((1 - mp) * 256, 256), 256)
    own_rows = pl.ds(mp * 4, 4)
    s0 = go(g.at[:, :, 1 - core], r0, sibling)
    late = [
        go(gf.at[:, :, :, away], gfo.at[own_rows], near),
        go(r.at[:, :, :, away], ro.at[own_rows], near),
    ]
    for n, (src, dst) in enumerate(((r, ro), (gf, gfo))):
        copy = pltpu.make_async_copy(src.at[:, :, :, lanes], dst.at[own_rows], local.at[n])
        copy.start()
        late.append(copy)
    s0.wait()

    ways = ((y, along_y, z, along_z), (z, along_z, y, along_y))

    def fold0(n, carry):
        block, part, a = n // 8, lax.rem(n // 4, 2), lax.rem(n, 4)
        mine = g[block, :, core, part, a].astype(F32)
        a0[block, :, part, a] = (mine + r0[block, :, part, a].astype(F32)).astype(BF)
        return carry

    lax.fori_loop(0, 16, fold0, 0)
    s1 = []
    for part, (ia, along_a, ib, along_b) in enumerate(ways):
        for step in (1, 2, 3):
            to = lax.rem(ia + step, 4)
            s1.append(go(a0.at[:, :, part, to], r1.at[part, step - 1], along_a(step)))
    for copy in s1:
        copy.wait()
    for part, (ia, along_a, ib, along_b) in enumerate(ways):

        def fold1(b, carry):
            total = a0[:, :, part, ia, b].astype(F32)
            for k in range(3):
                total = total + r1[part, k, :, :, b].astype(F32)
            a1[:, :, part, b] = total.astype(BF)
            return carry

        lax.fori_loop(0, 4, fold1, 0)
    s2 = []
    for part, (ia, along_a, ib, along_b) in enumerate(ways):
        for step in (1, 2, 3):
            to = lax.rem(ib + step, 4)
            s2.append(go(a1.at[:, :, part, to], r2.at[part, step - 1], along_b(step)))
    for copy in s2:
        copy.wait()
    for part, (ia, along_a, ib, along_b) in enumerate(ways):
        total = a1[:, :, part, ib].astype(F32)
        for k in range(3):
            total = total + r2[part, k].astype(F32)
        a2[:, :, part] = total.astype(BF)
    s3 = [
        go(a2.at[:, 1 - mp, :, x_hi], r3.at[0], near),
        go(a2.at[:, 1 - mp, :, 1 - x_hi], r3.at[1], far),
        go(a2.at[:, mp, :, 1 - x_hi], r3.at[2], opposite),
    ]
    for copy in s3:
        copy.wait()
    total = a2[:, mp, :, x_hi].astype(F32)
    for k in range(3):
        total = total + r3[k].astype(F32)
    total = total.astype(BF)
    for part, (ia, along_a, ib, along_b) in enumerate(ways):
        f[core, part, ia, ib, x_hi] = total[:, part]
    s4 = []
    for part, (ia, along_a, ib, along_b) in enumerate(ways):
        spot = f.at[core, part, ia, ib, x_hi]
        s4.append(go(spot, spot, opposite))
    for copy in s4:
        copy.wait()
    s5 = []
    for part, (ia, along_a, ib, along_b) in enumerate(ways):
        spot = f.at[core, part, ia, ib]
        for step in (1, 2, 3):
            s5.append(go(spot, spot, along_b(step)))
    for copy in s5:
        copy.wait()
    s6 = []
    for part, (ia, along_a, ib, along_b) in enumerate(ways):
        spot = f.at[core, part, ia]
        for step in (1, 2, 3):
            s6.append(go(spot, spot, along_a(step)))
    for copy in s6:
        copy.wait()
    spot = f.at[core]
    s7 = go(spot, spot, sibling)
    s7.wait()

    factor = 1.0 / 256.0

    def spread(n, carry):
        half, part, a = n // 8, lax.rem(n // 4, 2), lax.rem(n, 4)
        value = f[half, part, a].astype(F32) * factor
        for block in range(2):
            out[block, half, part, a] = value[:, :, block]
        return carry

    lax.fori_loop(0, 16, spread, 0)
    for copy in late:
        copy.wait()


NN = (((1,), (0,)), ((), ()))
NT = (((1,), (1,)), ((), ()))
TN = (((0,), (0,)), ((), ()))


def dot(left, right, dims=NN):
    return lax.dot_general(left, right, dims, preferred_element_type=F32)


def head_masks():
    lane = lax.broadcasted_iota(jnp.int32, (128, 128), 1) // HEAD_DIM
    return [lane == h for h in range(4)]


def spread_heads(block, masks):
    zero = jnp.zeros_like(block)
    return jnp.concatenate([jnp.where(m, block, zero) for m in masks], 0)


def merge_heads(tall, masks):
    total = jnp.where(masks[0], tall[0:128], 0.0)
    for h in range(1, 4):
        total = jnp.where(masks[h], tall[h * 128 : (h + 1) * 128], total)
    return total


def standardize(x):
    centred = x - jnp.mean(x, -1, keepdims=True)
    inv = lax.rsqrt(jnp.mean(centred * centred, -1, keepdims=True) + 1e-05)
    return centred * inv, inv


def window(ref, w, offset):
    i, j = w // 2, lax.rem(w, 2)
    got = ref[pl.ds(2 * i + offset, 2), pl.ds(2 * j + offset, 2)]
    return got.reshape(128, D)


def put_window(ref, w, value):
    i, j = w // 2, lax.rem(w, 2)
    ref[pl.ds(2 * i, 2), pl.ds(2 * j, 2)] = value.reshape(2, 2, 32, D)


def forward(x, offset, wq, wo, n, pr, es, rd, mix, out, cut):
    def norm(w, carry):
        n[w] = standardize(window(x, w, offset).astype(F32))[0].astype(BF)
        return carry

    lax.fori_loop(0, 4, norm, 0)
    for c in range(3):
        for j in range(2):
            got = dot(n[...].reshape(512, 512), wq[c, :, j * 256 : (j + 1) * 256])
            pr[:, :, c * 512 + j * 256 : c * 512 + (j + 1) * 256] = got.astype(BF).reshape(4, 128, 256)

    masks = head_masks()
    ones = spread_heads(jnp.ones((128, 128), BF), masks)
    if cut is not None:
        q_half = lax.broadcasted_iota(jnp.int32, (128, 512), 0) // 64
        k_half = lax.rem(lax.broadcasted_iota(jnp.int32, (128, 512), 1) // 64, 2)
        same = q_half == k_half

    def attend(w, carry):
        for s in range(4):
            q = pr[w, :, s * 128 : (s + 1) * 128]
            k = spread_heads(pr[w, :, 512 + s * 128 : 512 + (s + 1) * 128], masks)
            v = spread_heads(pr[w, :, 1024 + s * 128 : 1024 + (s + 1) * 128], masks)
            e = jnp.exp2(dot(q, k, NT) * (SCALE * LOG2E))
            if cut is not None:
                e = jnp.where(same | jnp.logical_not(cut & (w >= 2)), e, 0.0)
            e = e.astype(BF)
            es[w, s] = e
            both = dot(e, jnp.concatenate([v, ones], 1))
            inv = 1.0 / both[:, 128:]
            rd[w, :, s * 128 : (s + 1) * 128] = inv
            mix[w, :, s * 128 : (s + 1) * 128] = (both[:, :128] * inv).astype(BF)
        return carry

    lax.fori_loop(0, 4, attend, 0)

    def project(w, carry):
        value = window(x, w, offset).astype(F32) + dot(mix[w], wo[...])
        put_window(out, w, value.astype(BF))
        return carry

    lax.fori_loop(0, 4, project, 0)


def backward(x, offset, ct, ct_offset, wq, wo, n, pr, es, rd, mix, cw, do, dpr, out, g):
    def gather(w, carry):
        cw[w] = window(ct, w, ct_offset)
        return carry

    lax.fori_loop(0, 4, gather, 0)
    for j in range(2):
        cols = slice(j * 256, (j + 1) * 256)
        got = dot(cw[...].reshape(512, 512), wo[cols, :], NT)
        do[:, :, cols] = got.reshape(4, 128, 256)
        got = dot(mix[:, :, cols].reshape(512, 256), cw[...].reshape(512, 512), TN).astype(BF)
        g[j, 1536:1792] = got[:, 0:256]
        g[j, 1792:2048] = got[:, 256:512]

    masks = head_masks()
    ones = spread_heads(jnp.ones((128, 128), BF), masks)

    def attend(w, carry):
        for s in range(4):
            lanes = slice(s * 128, (s + 1) * 128)
            q = pr[w, :, lanes]
            k = spread_heads(pr[w, :, 512 + s * 128 : 512 + (s + 1) * 128], masks)
            v = spread_heads(pr[w, :, 1024 + s * 128 : 1024 + (s + 1) * 128], masks)
            e = es[w, s]
            g1 = do[w, :, lanes] * rd[w, :, lanes]
            g2 = g1 * mix[w, :, lanes].astype(F32)
            g1 = g1.astype(BF)
            t = dot(jnp.concatenate([g1, (-g2).astype(BF)], 1), jnp.concatenate([v, ones], 1), NT)
            ds = (e.astype(F32) * t).astype(BF)
            dq = dot(ds, k) * SCALE
            dk = merge_heads(dot(ds, q, TN), masks) * SCALE
            dv = merge_heads(dot(e, g1, TN), masks)
            dpr[w, :, lanes] = dq.astype(BF)
            dpr[w, :, 512 + s * 128 : 512 + (s + 1) * 128] = dk.astype(BF)
            dpr[w, :, 1024 + s * 128 : 1024 + (s + 1) * 128] = dv.astype(BF)
        return carry

    lax.fori_loop(0, 4, attend, 0)
    for c in range(3):
        for j in range(2):
            cols = slice(c * 512 + j * 256, c * 512 + (j + 1) * 256)
            got = dot(n[...].reshape(512, 512), dpr[:, :, cols].reshape(512, 256), TN)
            g[j, c * 512 : (c + 1) * 512] = got.astype(BF)

    def finish(w, carry):
        grad = dot(dpr[w, :, 0:512], wq[0], NT)
        grad = grad + dot(dpr[w, :, 512:1024], wq[1], NT)
        grad = grad + dot(dpr[w, :, 1024:1536], wq[2], NT)
        standard, inv = standardize(window(x, w, offset).astype(F32))
        back = inv * (
            grad
            - jnp.mean(grad, -1, keepdims=True)
            - standard * jnp.mean(grad * standard, -1, keepdims=True)
        )
        put_window(out, w, (cw[w].astype(F32) + back).astype(BF))
        return carry

    lax.fori_loop(0, 4, finish, 0)


def plain_forward_kernel(x, wq, wo, out, n, pr, es, rd, mix):
    forward(x, 0, wq, wo, n, pr, es, rd, mix, out, None)


def shift_kernel(x, ct, wq, wo, out, back, g, n, pr, es, rd, mix, cw, do, dpr):
    lat, lon, mp = place()
    cut = (lat * 2 + mp) == 15
    forward(x, 1, wq, wo, n, pr, es, rd, mix, out, cut)
    backward(x, 1, ct, 1, wq, wo, n, pr, es, rd, mix, cw, do, dpr, back, g)


def plain_backward_kernel(x, ct, wq, wo, n, pr, es, rd, mix, back, g, cw, do, dpr):
    backward(x, 0, ct, 0, wq, wo, n, pr, es, rd, mix, cw, do, dpr, back, g)


def shape(*dims, dtype=BF):
    return jax.ShapeDtypeStruct(dims, dtype)


SAVED = ((4, 128, 512), BF), ((4, 128, 1536), BF), ((4, 4, 128, 512), BF), ((4, 128, 512), F32), ((4, 128, 512), BF)
WORK = ((4, 128, 512), BF), ((4, 128, 512), F32), ((4, 128, 1536), BF)


def compute_call(kernel, out_shape, scratch=()):
    vmem = pl.BlockSpec(memory_space=pltpu.VMEM)

    def call(*args):
        return pl.pallas_call(
            kernel,
            out_shape=out_shape,
            in_specs=[vmem] * len(args),
            out_specs=[vmem] * len(out_shape),
            scratch_shapes=[pltpu.VMEM(s, t) for s, t in scratch],
            compiler_params=pltpu.CompilerParams(vmem_limit_bytes=VMEM_LIMIT),
        )(*args)

    return call


def cells(tokens):
    return tokens.reshape(8, 4, 4, 8, 256).transpose(0, 2, 1, 3, 4).reshape(8, 4, 32, 256)


def uncells(tokens):
    return tokens.reshape(8, 4, 4, 8, 256).transpose(0, 2, 1, 3, 4).reshape(32, 32, 256)


def on_device(fields, qkv_plain, out_plain, qkv_shift, out_shift, cotangent):
    grid = shape(4, 4, 32, 512)
    wide = shape(5, 5, 32, 512)
    wq, wo = shape(3, 512, 512), shape(512, 512)
    x, c, wqp, wop, wqs, wos = comm_call(
        enter_kernel, [grid, grid, wq, wo, wq, wo], 18, 0, locals_=6
    )(
        cells(fields),
        cells(cotangent),
        qkv_plain.transpose(1, 0, 2),
        out_plain,
        qkv_shift.transpose(1, 0, 2),
        out_shift,
    )
    hidden, *saved = compute_call(
        plain_forward_kernel, [grid] + [shape(*s, dtype=t) for s, t in SAVED]
    )(x, wqp, wop)
    hx, cx = comm_call(widen_kernel, [wide, wide], 6, 1, locals_=2)(hidden, c)
    grads = shape(2, 2048, 256)
    shifted_result, shifted_grad, g_shift = compute_call(
        shift_kernel, [grid, grid, grads], SAVED + WORK
    )(hx, cx, wqs, wos)
    result, grad_hidden = comm_call(narrow_kernel, [grid, grid], 6, 2, locals_=2)(
        shifted_result, shifted_grad
    )
    grad_fields, g_plain = compute_call(plain_backward_kernel, [grid, grads], WORK)(
        x, grad_hidden, wqp, wop, *saved
    )
    g = jnp.stack([g_plain, g_shift]).reshape(2, 2, 2, 2, 4, 4, 2, 16, 256)
    held = shape(8, 4, 32, 256)
    result, grad_fields, sums = comm_call(
        leave_kernel,
        [held, held, shape(2, 2, 2, 4, 4, 2, 16, 256, dtype=F32)],
        34,
        3,
        scratch=(
            pltpu.VMEM((2, 2, 2, 4, 4, 2, 16, 256), BF),
            pltpu.VMEM((2, 2, 2, 4, 4, 2, 16, 256), BF),
            pltpu.VMEM((2, 3, 2, 2, 4, 2, 16, 256), BF),
            pltpu.VMEM((2, 2, 2, 4, 2, 16, 256), BF),
            pltpu.VMEM((2, 3, 2, 2, 2, 16, 256), BF),
            pltpu.VMEM((2, 2, 2, 2, 16, 256), BF),
            pltpu.VMEM((3, 2, 2, 16, 256), BF),
            pltpu.VMEM((2, 2, 4, 4, 2, 2, 16, 256), BF),
        ),
        locals_=2,
    )(result, grad_fields, g)
    sums = sums.reshape(2, 2048, 256)
    outs = []
    for block in range(2):
        outs.append(sums[block, :1536].reshape(3, 512, 256).transpose(1, 0, 2))
        outs.append(jnp.concatenate([sums[block, 1536:1792], sums[block, 1792:]], 1))
    return (uncells(result), uncells(grad_fields), *outs)


def solution(mesh):
    in_specs = (
        P("lat", "lon", "mp"),
        P(None, None, "mp"),
        P("mp", None),
        P(None, None, "mp"),
        P("mp", None),
        P("lat", "lon", "mp"),
    )
    out_specs = (
        P("lat", "lon", "mp"),
        P("lat", "lon", "mp"),
        P(None, None, "mp"),
        P("mp", None),
        P(None, None, "mp"),
        P("mp", None),
    )
    return jax.shard_map(
        on_device, mesh=mesh, in_specs=in_specs, out_specs=out_specs, check_vma=False
    )
```

time: 1030 us -> 176 us (0.17)
  waiting for transfers between devices: 804 us -> 0 us
  Pallas kernels: 0 us -> 160 us
  matrix products: 77 us -> 0 us
  local copies, waits for them, and re-layouts: 85.1 us -> 9.37 us
  other arithmetic: 31.1 us -> 5.65 us
  starting transfers between devices: 15.4 us -> 0 us
  between operations: 14.8 us -> 0.7 us
    psum x1 -> x0, waiting for transfers between devices: 651 us -> none  [on_device(): lax.psum((gradients[0], gradients[1], gradients[2], gradients[3]), ('lat'...]
    pallas_call x0 -> x7, Pallas kernels: none -> 160 us  [call(): pl.pallas_call(kernel, out_shape=out_shape, in_specs=[vmem] * len(args),...]
    all_gather x4 -> x0, waiting for transfers between devices: 77.5 us -> none  [assemble(): return lax.all_gather(shard, 'mp', axis=2, tiled=True)]
    dot_general x24 -> x0, matrix products: 77 us -> none  [the longest x6 25.9 us: attention_core(): jnp.einsum('wqhe,wkhe->whqk', queries, key_part, preferred_element_type=j...]
    reduce_scatter x4 -> x0, waiting for transfers between devices: 65.9 us -> none  [reduce_heads(): lax.psum_scatter(term.astype(jnp.bfloat16), 'mp', scatter_dimension=2, ti...]
    dot_general x4 -> x0, local copies, waits for them, and re-layouts: 30.4 us -> none  [the longest x2 23.1 us: group_backward(): jnp.einsum('wtce,dce->wtd', grad_projected, qkv_weight, preferred_element...]
    convert_element_type x12 -> x0, other arithmetic: 16.8 us -> none  [the longest x2 4.64 us: reduce_heads(): term.astype(jnp.bfloat16)]
    add_any x2 -> x0, local copies, waits for them, and re-layouts: 16.5 us -> none  [attention_core(): blocked[:, :, 0]]
  transfers between devices with their start and end apart: 17 -> 0, of which waited for: 12 -> 0; matrix products, arithmetic and copies ran while one was open for 7% -> 0% of each run, Pallas kernels for 0% -> 0%
where the time goes in v1:
time: 176 us; the launch traced here: 175 us
  Pallas kernels  160 us (91%)
  local copies, waits for them, and re-layouts  9.37 us (5%)
  other arithmetic  5.65 us (3%)
    pallas_call x7, Pallas kernels, call(): pl.pallas_call(kernel, out_shape=out_shape, in_specs=[vmem] * len(args),...  160 us
    transpose x2, local copies, waits for them, and re-layouts, uncells(): tokens.reshape(8, 4, 4, 8, 256).transpose(0, 2, 1, 3, 4)  3.94 us
    another operation x1, other arithmetic, on_device(): g = jnp.stack([g_plain, g_shift]).reshape(2, 2, 2, 2, 4, 4, 2, 16, 256)  3.93 us

profile of v1, /device:TPU:1, one launch (start us, length us, event | category | flops | bytes accessed | tf_op | source)
XLA Modules:
  0.0 175.5 jit_solution(277204100132864228)
XLA Ops:
  0.6 2.3 %copy_bitcast_fusion = (bf16[8,4,32,256]{3,2,1,0:T(8,128)(2,1)}, bf16[8,4,32,256]{3,2,1,0:T(8,128)(2,1)}) fusion(bf16[8,4,4,8,256]{4,3,2,1,0:T(8,128)(2,1)} %bitcast.49, bf16[8,4,4,8,256]{4,3,2,1,0:T(8,128)(2,1)} %bitcast.50), kind=kLoop, calls=%fused_computation.3 | loop fusion | bytes 2097152 | tf_op jit(solution)/shard_map/reshape | solution.py:492
  2.9 30.5 %shard_map.109 = (bf16[4,4,32,512]{3,2,1,0:T(8,128)(2,1)}, bf16[4,4,32,512]{3,2,1,0:T(8,128)(2,1)}, bf16[3,512,512]{2,1,0:T(8,128)(2,1)}, bf16[512,512]{1,0:T(8,...) custom-call(bf16[8,4,32,256]{3,2,1,0:T(8,128)(2,1)} %get-tuple-element.61.fc, ...), custom_call_target="tpu_custom_call" | custom-call | tf_op jit(solution)/shard_map/pallas_call | solution.py:59
  33.4 9.1 %shard_map.110 = (bf16[4,4,32,512]{3,2,1,0:T(8,128)(2,1)}, bf16[4,128,512]{2,1,0:T(8,128)(2,1)}, bf16[4,128,1536]{2,1,0:T(8,128)(2,1)}, bf16[4,4,128,512]{3,2,1,...) custom-call(bf16[4,4,32,512]{3,2,1,0:T(8,128)(2,1)} %get-tuple-element.30.x, ...), custom_call_target="tpu_custom_call" | custom-call | tf_op jit(solution)/shard_map/pallas_call | solution.py:479
  42.5 15.6 %shard_map.111 = (bf16[5,5,32,512]{3,2,1,0:T(8,128)(2,1)}, bf16[5,5,32,512]{3,2,1,0:T(8,128)(2,1)}) custom-call(bf16[4,4,32,512]{3,2,1,0:T(8,128)(2,1)} %get-tuple-element.33.h, bf16[4,4,32,512]{3,2,1,0:T(8,128)(2,1)} %get-tuple-element.34.c), custom_call_target="tpu_custom_call" | custom-call | tf_op jit(solution)/shard_map/pallas_call | solution.py:59
  58.2 18.7 %shard_map.112 = (bf16[4,4,32,512]{3,2,1,0:T(8,128)(2,1)}, bf16[4,4,32,512]{3,2,1,0:T(8,128)(2,1)}, bf16[2,2048,256]{2,1,0:T(8,128)(2,1)}) custom-call(bf16[5,5,32,512]{3,2,1,0:T(8,128)(2,1)} %get-tuple-element.35.x, bf16[5,5,32,512]{3,2,1,0:T(8,128)(2,1)} %get-tuple-element.36.ct, bf16[3,512,512]{2,1,0:T(8,128)(2,1)} %get-tuple-element.37.wq, ...), custom_call_target="tpu_custom_call" | custom-call | tf_op jit(solution)/shard_map/pallas_call | solution.py:479
  76.8 16.3 %shard_map.113 = (bf16[4,4,32,512]{3,2,1,0:T(8,128)(2,1)}, bf16[4,4,32,512]{3,2,1,0:T(8,128)(2,1)}) custom-call(bf16[4,4,32,512]{3,2,1,0:T(8,128)(2,1)} %get-tuple-element.39.a, bf16[4,4,32,512]{3,2,1,0:T(8,128)(2,1)} %get-tuple-element.40.b), custom_call_target="tpu_custom_call" | custom-call | tf_op jit(solution)/shard_map/pallas_call | solution.py:59
  93.1 0.0 copy-start.1
  93.1 14.5 %shard_map.114 = (bf16[4,4,32,512]{3,2,1,0:T(8,128)(2,1)}, bf16[2,2048,256]{2,1,0:T(8,128)(2,1)}) custom-call(bf16[4,4,32,512]{3,2,1,0:T(8,128)(2,1)} %get-tuple-element.30.x, bf16[4,4,32,512]{3,2,1,0:T(8,128)(2,1)} %get-tuple-element.42.ct, bf16[3,512,512]{2,1,0:T(8,128)(2,1)} %get-tuple-element.31.wq, bf16[512,512]{1,0:T(8,128)(2,1)} %get-tuple-element.32.wo, ...), custom_call_target="tpu_custom_call" | custom-call | tf_op jit(solution)/shard_map/pallas_call | solution.py:479
  107.6 0.0 copy-done.1
  107.6 3.9 %pad_maximum_fusion.g = bf16[2,2,2,2,4,4,2,16,256]{8,7,6,5,4,3,2,1,0:T(8,128)(2,1)} fusion(bf16[1,2,2,2,4,4,2,16,256]{8,7,6,5,4,3,2,1,0:T(8,128)(2,1)S(1)} %bitcast.39, bf16[1,2,2,2,4,4,2,16,256]{8,7,6,5,4,3,2,1,0:T(8,128)(2,1)} %bitcast.40), kind=kLoop, calls=%fused_computation | loop fusion | flops 2097152 | bytes 8388608 | tf_op jit(solution)/shard_map/stack | solution.py:527
  111.5 55.1 %shard_map.115 = (bf16[8,4,32,256]{3,2,1,0:T(8,128)(2,1)}, bf16[8,4,32,256]{3,2,1,0:T(8,128)(2,1)}, f32[2,2,2,4,4,2,16,256]{7,6,5,4,3,2,1,0:T(8,128)}) custom-call(bf16[4,4,32,512]{3,2,1,0:T(8,128)(2,1)} %get-tuple-element.41.r, bf16[4,4,32,512]{3,2,1,0:T(8,128)(2,1)} %get-tuple-element.48.gf, bf16[2,2,2,2,4,4,2,16,256]{8,7,6,5,4,3,2,1,0:T(8,128)(2,1)} %pad_maximum_fusion.g), custom_call_target="tpu_custom_call" | custom-call | tf_op jit(solution)/shard_map/pallas_call | solution.py:59
  166.6 0.0 copy-start
  166.7 2.0 %copy.14 = bf16[8,4,4,8,256]{4,3,2,1,0:T(8,128)(2,1)} copy(bf16[8,4,4,8,256]{4,3,1,2,0:T(8,128)(2,1)} %bitcast.48) | data formatting | bytes 1048576 | tf_op jit(solution)/shard_map/transpose | solution.py:496
  168.7 1.9 %copy.15 = bf16[8,4,4,8,256]{4,3,2,1,0:T(8,128)(2,1)} copy(bf16[8,4,4,8,256]{4,3,1,2,0:T(8,128)(2,1)} %bitcast.47) | data formatting | bytes 1048576 | tf_op jit(solution)/shard_map/transpose | solution.py:496
  170.6 1.3 slice_bitcast_fusion.1
  171.9 0.0 copy-done
  171.9 1.9 %fusion = (f32[1,1536,256]{2,1,0:T(8,128)}, f32[1,1536,256]{2,1,0:T(8,128)}) fusion(f32[2,2048,256]{2,1,0:T(8,128)S(1)} %bitcast.38), kind=kLoop, calls=%fused_computation.9 | loop fusion | bytes 6291456 | tf_op jit(solution)/shard_map/slice | solution.py:549
  173.7 0.9 pad_maximum_fusion.2
  174.6 0.9 pad_maximum_fusion.1
Async XLA Ops:
  93.1 14.5 %copy-start.1 = (bf16[2,2048,256]{2,1,0:T(8,128)(2,1)S(1)}, bf16[2,2048,256]{2,1,0:T(8,128)(2,1)}, u32[]{:S(2)}) copy-start(bf16[2,2048,256]{2,1,0:T(8,128)(2,1)} %get-tuple-element.50) | copy-start | bytes 6291460
  166.6 5.2 %copy-start = (f32[2,2,2,4,4,2,16,256]{7,6,5,4,3,2,1,0:T(8,128)S(1)}, f32[2,2,2,4,4,2,16,256]{7,6,5,4,3,2,1,0:T(8,128)}, u32[]{:S(2)}) copy-start(f32[2,2,2,4,4,2,16,256]{7,6,5,4,3,2,1,0:T(8,128)} %get-tuple-element.53) | copy-start | bytes 12582916

commit v2 on v1

v2 whole, which is shorter than its diff:
```python
import functools

import jax
import jax.numpy as jnp
from jax import lax
from jax.experimental import pallas as pl
from jax.experimental.pallas import tpu as pltpu
from jax.sharding import PartitionSpec as P

BF = jnp.bfloat16
F32 = jnp.float32
MESH = pl.DeviceIdType.MESH
VMEM_LIMIT = 56 * 1024 * 1024
D = 512
HEAD_DIM = 32
SCALE = HEAD_DIM ** -0.5
LOG2E = 1.4426950408889634


def place():
    lat, lon, mp = lax.axis_index("lat"), lax.axis_index("lon"), lax.axis_index("mp")
    return lat, lon, mp


def row_step(lat, mp, step):
    at = lax.rem(lat * 2 + mp + step + 16, 16)
    return at // 2, lax.rem(at, 2)


def barrier(peers):
    sem = pltpu.get_barrier_semaphore()
    for peer in peers:
        pl.semaphore_signal(sem, inc=1, device_id=peer, device_id_type=MESH)
    pl.semaphore_wait(sem, len(peers))


class Sender:
    def __init__(self, send, recv):
        self.send, self.recv, self.used = send, recv, 0

    def __call__(self, src, dst, peer):
        copy = pltpu.make_async_remote_copy(
            src_ref=src,
            dst_ref=dst,
            send_sem=self.send.at[self.used],
            recv_sem=self.recv.at[self.used],
            device_id=peer,
            device_id_type=MESH,
        )
        self.used += 1
        copy.start()
        return copy


NN = (((1,), (0,)), ((), ()))
NT = (((1,), (1,)), ((), ()))
TN = (((0,), (0,)), ((), ()))


def dot(left, right, dims=NN):
    return lax.dot_general(left, right, dims, preferred_element_type=F32)


def head_masks():
    lane = lax.broadcasted_iota(jnp.int32, (128, 128), 1) // HEAD_DIM
    return [lane == h for h in range(4)]


def spread_heads(block, masks):
    zero = jnp.zeros_like(block)
    return jnp.concatenate([jnp.where(m, block, zero) for m in masks], 0)


def merge_heads(tall, masks):
    total = jnp.where(masks[0], tall[0:128], 0.0)
    for h in range(1, 4):
        total = jnp.where(masks[h], tall[h * 128 : (h + 1) * 128], total)
    return total


def standardize(x):
    centred = x - jnp.mean(x, -1, keepdims=True)
    inv = lax.rsqrt(jnp.mean(centred * centred, -1, keepdims=True) + 1e-05)
    return centred * inv, inv


def window(ref, w, offset):
    i, j = w // 2, lax.rem(w, 2)
    got = ref[pl.ds(2 * i + offset, 2), pl.ds(2 * j + offset, 2)]
    return got.reshape(128, D)


def put_window(ref, w, value):
    i, j = w // 2, lax.rem(w, 2)
    ref[pl.ds(2 * i, 2), pl.ds(2 * j, 2)] = value.reshape(2, 2, 32, D)


def forward_norm(x, offset, n, low, high):
    def norm(w, carry):
        n[w] = standardize(window(x, w, offset).astype(F32))[0].astype(BF)
        return carry

    lax.fori_loop(low, high, norm, 0)


def forward_project(n, wq, pr, low, high):
    count = high - low
    for c in range(3):
        for j in range(2):
            cols = slice(c * 512 + j * 256, c * 512 + (j + 1) * 256)
            got = dot(n[low:high].reshape(count * 128, 512), wq[c, :, j * 256 : (j + 1) * 256])
            pr[low:high, :, cols] = got.astype(BF).reshape(count, 128, 256)


def forward_attend(pr, es, rd, mix, cut, low, high):
    masks = head_masks()
    ones = spread_heads(jnp.ones((128, 128), BF), masks)
    if cut is not None:
        q_half = lax.broadcasted_iota(jnp.int32, (128, 512), 0) // 64
        k_half = lax.rem(lax.broadcasted_iota(jnp.int32, (128, 512), 1) // 64, 2)
        same = q_half == k_half

    def attend(w, carry):
        for s in range(4):
            q = pr[w, :, s * 128 : (s + 1) * 128]
            k = spread_heads(pr[w, :, 512 + s * 128 : 512 + (s + 1) * 128], masks)
            v = spread_heads(pr[w, :, 1024 + s * 128 : 1024 + (s + 1) * 128], masks)
            e = jnp.exp2(dot(q, k, NT) * (SCALE * LOG2E))
            if cut is not None:
                e = jnp.where(same | jnp.logical_not(cut & (w >= 2)), e, 0.0)
            e = e.astype(BF)
            es[w, s] = e
            both = dot(e, jnp.concatenate([v, ones], 1))
            inv = 1.0 / both[:, 128:]
            rd[w, :, s * 128 : (s + 1) * 128] = inv
            mix[w, :, s * 128 : (s + 1) * 128] = (both[:, :128] * inv).astype(BF)
        return carry

    lax.fori_loop(low, high, attend, 0)


def forward_out(x, offset, wo, mix, out, low, high):
    def project(w, carry):
        value = window(x, w, offset).astype(F32) + dot(mix[w], wo[...])
        put_window(out, w, value.astype(BF))
        return carry

    lax.fori_loop(low, high, project, 0)


def backward_out(ct, ct_offset, wo, mix, cw, do, g):
    def gather(w, carry):
        cw[w] = window(ct, w, ct_offset)
        return carry

    lax.fori_loop(0, 4, gather, 0)
    for j in range(2):
        cols = slice(j * 256, (j + 1) * 256)
        got = dot(cw[...].reshape(512, 512), wo[cols, :], NT)
        do[:, :, cols] = got.reshape(4, 128, 256)
    for j in range(2):
        cols = slice(j * 256, (j + 1) * 256)
        got = dot(mix[:, :, cols].reshape(512, 256), cw[...].reshape(512, 512), TN).astype(BF)
        g[j, 1, 1, 0:2] = got[:, 0:256].reshape(2, 4, 2, 16, 256)
        g[j, 1, 1, 2:4] = got[:, 256:512].reshape(2, 4, 2, 16, 256)


def backward_attend(pr, es, rd, mix, do, dpr, low, high):
    masks = head_masks()
    ones = spread_heads(jnp.ones((128, 128), BF), masks)

    def attend(w, carry):
        for s in range(4):
            lanes = slice(s * 128, (s + 1) * 128)
            q = pr[w, :, lanes]
            k = spread_heads(pr[w, :, 512 + s * 128 : 512 + (s + 1) * 128], masks)
            v = spread_heads(pr[w, :, 1024 + s * 128 : 1024 + (s + 1) * 128], masks)
            e = es[w, s]
            g1 = do[w, :, lanes] * rd[w, :, lanes]
            g2 = g1 * mix[w, :, lanes].astype(F32)
            g1 = g1.astype(BF)
            t = dot(jnp.concatenate([g1, (-g2).astype(BF)], 1), jnp.concatenate([v, ones], 1), NT)
            ds = (e.astype(F32) * t).astype(BF)
            dq = dot(ds, k) * SCALE
            dk = merge_heads(dot(ds, q, TN), masks) * SCALE
            dv = merge_heads(dot(e, g1, TN), masks)
            dpr[w, :, lanes] = dq.astype(BF)
            dpr[w, :, 512 + s * 128 : 512 + (s + 1) * 128] = dk.astype(BF)
            dpr[w, :, 1024 + s * 128 : 1024 + (s + 1) * 128] = dv.astype(BF)
        return carry

    lax.fori_loop(low, high, attend, 0)


def backward_weights(n, dpr, g):
    for c in range(3):
        for j in range(2):
            cols = slice(c * 512 + j * 256, c * 512 + (j + 1) * 256)
            got = dot(n[...].reshape(512, 512), dpr[:, :, cols].reshape(512, 256), TN)
            g[j, c // 2, c % 2] = got.astype(BF).reshape(4, 4, 2, 16, 256)


def backward_tokens(x, offset, wq, cw, dpr, out):
    def finish(w, carry):
        grad = dot(dpr[w, :, 0:512], wq[0], NT)
        grad = grad + dot(dpr[w, :, 512:1024], wq[1], NT)
        grad = grad + dot(dpr[w, :, 1024:1536], wq[2], NT)
        standard, inv = standardize(window(x, w, offset).astype(F32))
        back = inv * (
            grad
            - jnp.mean(grad, -1, keepdims=True)
            - standard * jnp.mean(grad * standard, -1, keepdims=True)
        )
        put_window(out, w, (cw[w].astype(F32) + back).astype(BF))
        return carry

    lax.fori_loop(0, 4, finish, 0)


class Sum:
    def __init__(self, go, g, f, r0, a0, r1, a1, r2, a2, r3):
        self.go, self.g, self.f = go, g, f
        self.r0, self.a0, self.r1, self.a1, self.r2, self.a2, self.r3 = r0, a0, r1, a1, r2, a2, r3
        lat, lon, mp = place()
        self.mp, self.core, z = mp, lax.rem(lon, 2), lon // 2
        y, self.x_hi = lax.rem(lat, 4), lat // 4
        self.near = (lat, lon, 1 - mp)
        self.far = (lax.rem(lat + 4, 8), lon, 1 - mp)
        self.opposite = (lax.rem(lat + 4, 8), lon, mp)
        self.sibling = (lat, lon + 1 - 2 * self.core, mp)

        def along_y(step):
            return (lat // 4 * 4 + lax.rem(y + step, 4), lon, mp)

        def along_z(step):
            return (lat, lax.rem(z + step, 4) * 2 + lax.rem(lon, 2), mp)

        self.ways = ((y, along_y, z, along_z), (z, along_z, y, along_y))
        self.peers = [self.near, self.far, self.opposite, self.sibling]
        self.peers += [along_y(s) for s in (1, 2, 3)] + [along_z(s) for s in (1, 2, 3)]
        self.flying = []

    def wait(self):
        for copy in self.flying:
            copy.wait()
        self.flying = []

    def step0(self):
        self.flying = [self.go(self.g.at[:, 1 - self.core], self.r0, self.sibling)]

    def step1(self):
        self.wait()
        g, r0, a0, core = self.g, self.r0, self.a0, self.core

        def fold(n, carry):
            part, a = n // 4, lax.rem(n, 4)
            mine = g[:, core, part, a].astype(F32)
            a0[:, part, a] = (mine + r0[:, part, a].astype(F32)).astype(BF)
            return carry

        lax.fori_loop(0, 8, fold, 0)
        for step in (1, 2, 3):
            for part, (ia, along_a, ib, along_b) in enumerate(self.ways):
                to = lax.rem(ia + step, 4)
                self.flying.append(
                    self.go(a0.at[:, part, to], self.r1.at[part, step - 1], along_a(step))
                )

    def step2(self):
        self.wait()
        a0, r1, a1 = self.a0, self.r1, self.a1
        for part, (ia, along_a, ib, along_b) in enumerate(self.ways):

            def fold(b, carry):
                total = a0[:, part, ia, b].astype(F32)
                for k in range(3):
                    total = total + r1[part, k, :, b].astype(F32)
                a1[:, part, b] = total.astype(BF)
                return carry

            lax.fori_loop(0, 4, fold, 0)
        for step in (1, 2, 3):
            for part, (ia, along_a, ib, along_b) in enumerate(self.ways):
                to = lax.rem(ib + step, 4)
                self.flying.append(
                    self.go(a1.at[:, part, to], self.r2.at[part, step - 1], along_b(step))
                )

    def step3(self):
        self.wait()
        a1, r2, a2, r3, mp, x_hi = self.a1, self.r2, self.a2, self.r3, self.mp, self.x_hi
        for part, (ia, along_a, ib, along_b) in enumerate(self.ways):
            total = a1[:, part, ib].astype(F32)
            for k in range(3):
                total = total + r2[part, k].astype(F32)
            a2[:, part] = total.astype(BF)
        self.flying = [
            self.go(a2.at[1 - mp, :, x_hi], r3.at[0], self.near),
            self.go(a2.at[1 - mp, :, 1 - x_hi], r3.at[1], self.far),
            self.go(a2.at[mp, :, 1 - x_hi], r3.at[2], self.opposite),
        ]

    def step4(self):
        self.wait()
        total = self.a2[self.mp, :, self.x_hi].astype(F32)
        for k in range(3):
            total = total + self.r3[k].astype(F32)
        total = total.astype(BF)
        for part, (ia, along_a, ib, along_b) in enumerate(self.ways):
            self.f[self.core, part, ia, ib, self.x_hi] = total[part]
        for part, (ia, along_a, ib, along_b) in enumerate(self.ways):
            spot = self.f.at[self.core, part, ia, ib, self.x_hi]
            self.flying.append(self.go(spot, spot, self.opposite))

    def step5(self):
        self.wait()
        for step in (1, 2, 3):
            for part, (ia, along_a, ib, along_b) in enumerate(self.ways):
                spot = self.f.at[self.core, part, ia, ib]
                self.flying.append(self.go(spot, spot, along_b(step)))

    def step6(self):
        self.wait()
        for step in (1, 2, 3):
            for part, (ia, along_a, ib, along_b) in enumerate(self.ways):
                spot = self.f.at[self.core, part, ia]
                self.flying.append(self.go(spot, spot, along_a(step)))

    def step7(self):
        self.wait()
        spot = self.f.at[self.core]
        self.flying = [self.go(spot, spot, self.sibling)]


def around(lat, lon, mp, step):
    row_lat, row_mp = row_step(lat, mp, step)
    col = lax.rem(lon + step + 8, 8)
    return (row_lat, lon, row_mp), (lat, col, mp), (row_lat, col, row_mp)


SENDS = 112
NEAR_ROWS = (96, 256)


def pair_kernel(
    fc, cc, wqp, wop, wqs, wos,
    ro, gfo, f_plain, f_shift,
    x, hx, cx, rs, rp, gs, gp, gf,
    fqp, fop, fqs, fos,
    n_p, pr_p, es_p, rd_p, mix_p,
    n_s, pr_s, es_s, rd_s, mix_s,
    cw, do, dpr,
    g_plain, g_shift,
    *rest,
):
    sums, (send, recv, local) = rest[:14], rest[14:]
    lat, lon, mp = place()
    row_prev, col_prev, corner_prev = around(lat, lon, mp, -1)
    row_next, col_next, corner_next = around(lat, lon, mp, 1)
    go = Sender(send, recv)
    sum_plain = Sum(go, g_plain, f_plain, *sums[:7])
    sum_shift = Sum(go, g_shift, f_shift, *sums[7:])
    near, far, sibling, core = sum_plain.near, sum_plain.far, sum_plain.sibling, sum_plain.core
    barrier(
        sum_plain.peers
        + [row_prev, col_prev, corner_prev, row_next, col_next, corner_next]
    )
    lanes = pl.ds(pl.multiple_of(mp * 256, 256), 256)
    away = pl.ds(pl.multiple_of((1 - mp) * 256, 256), 256)
    other_rows = pl.ds((1 - mp) * 4, 4)
    own_rows = pl.ds(mp * 4, 4)
    own = pl.ds(0, 4)
    kept = []

    def keep(src, dst):
        copy = pltpu.make_async_copy(src, dst, local.at[len(kept)])
        copy.start()
        kept.append(copy)
        return copy

    def weight(src, dst, split):
        parts = []
        for k, (base, size) in enumerate(((0, split // 2), (split, (512 - split) // 2))):
            rows = pl.ds(pl.multiple_of(base + core * size, 16), size)
            copy = go(src.at[:, rows], dst.at[:, rows, lanes], (near, far)[k])
            parts.append((copy, dst.at[:, rows, away]))
        return parts

    def weight_out(src, dst):
        rows = pl.ds(pl.multiple_of(core * 128, 128), 128)
        there = pl.ds(pl.multiple_of(mp * 256 + core * 128, 128), 128)
        here = pl.ds(pl.multiple_of((1 - mp) * 256 + core * 128, 128), 128)
        return [(go(src.at[rows], dst.at[there], far), dst.at[here])]

    def pass_on(parts):
        shared = []
        for copy, spot in parts:
            copy.wait_recv()
            shared.append(go(spot, spot, sibling))
        return shared

    fields_copy = go(fc.at[other_rows], x.at[:, :, :, lanes], near)
    qkv_p = weight(wqp, fqp, NEAR_ROWS[0])
    out_p = weight_out(wop, fop)
    cot_copy = go(cc.at[other_rows], cx.at[own, own, :, lanes], near)
    qkv_s = weight(wqs, fqs, NEAR_ROWS[1])
    out_s = weight_out(wos, fos)
    mp_rows = pl.ds(pl.multiple_of(mp * 256, 256), 256)
    x_kept = keep(fc.at[own_rows], x.at[:, :, :, lanes])
    wq_kept = keep(wqp, fqp.at[:, :, lanes])
    others = [
        keep(wop, fop.at[mp_rows]),
        keep(cc.at[own_rows], cx.at[own, own, :, lanes]),
        keep(wqs, fqs.at[:, :, lanes]),
        keep(wos, fos.at[mp_rows]),
    ]

    fields_copy.wait()
    x_kept.wait()
    forward_norm(x, 0, n_p, 0, 4)
    shared = pass_on(qkv_p)
    wq_kept.wait()
    for copy in shared:
        copy.wait_recv()
    forward_project(n_p, fqp, pr_p, 0, 4)
    shared_out = pass_on(out_p)
    forward_attend(pr_p, es_p, rd_p, mix_p, None, 0, 4)
    for copy in others:
        copy.wait()
    for copy in shared_out:
        copy.wait_recv()
    forward_out(x, 0, fop, mix_p, hx, 0, 4)

    halos = [
        go(hx.at[0, own], hx.at[4, own], row_prev),
        go(hx.at[own, 0], hx.at[own, 4], col_prev),
        go(hx.at[0, 0], hx.at[4, 4], corner_prev),
    ]
    cot_copy.wait()
    cot_halos = [
        go(cx.at[0, own], cx.at[4, own], row_prev),
        go(cx.at[own, 0], cx.at[own, 4], col_prev),
        go(cx.at[0, 0], cx.at[4, 4], corner_prev),
    ]
    shared_s = pass_on(qkv_s)
    forward_norm(hx, 1, n_s, 0, 1)
    for copy in shared_s:
        copy.wait_recv()
    cut = (lat * 2 + mp) == 15
    forward_project(n_s, fqs, pr_s, 0, 1)
    shared_out_s = pass_on(out_s)
    forward_attend(pr_s, es_s, rd_s, mix_s, cut, 0, 1)
    for copy in halos:
        copy.wait()
    forward_norm(hx, 1, n_s, 1, 4)
    forward_project(n_s, fqs, pr_s, 1, 4)
    forward_attend(pr_s, es_s, rd_s, mix_s, cut, 1, 4)
    for copy in shared_out_s:
        copy.wait_recv()
    forward_out(hx, 1, fos, mix_s, rs, 0, 4)

    low, high = pl.ds(0, 3), pl.ds(1, 3)

    def narrow(src, dst):
        return [
            go(src.at[3, low], dst.at[0, high], row_next),
            go(src.at[low, 3], dst.at[high, 0], col_next),
            go(src.at[3, 3], dst.at[0, 0], corner_next),
            keep(src.at[low, low], dst.at[high, high]),
        ]

    result_halos = narrow(rs, rp)

    for copy in cot_halos:
        copy.wait()
    backward_out(cx, 1, fos, mix_s, cw, do, g_shift)
    backward_attend(pr_s, es_s, rd_s, mix_s, do, dpr, 0, 4)
    backward_tokens(hx, 1, fqs, cw, dpr, gs)
    grad_halos = narrow(gs, gp)
    for copy in result_halos:
        copy.wait()
    ends = [go(rp.at[:, :, :, away], ro.at[own_rows], near)]
    ends.append(keep(rp.at[:, :, :, lanes], ro.at[own_rows]))
    backward_weights(n_s, dpr, g_shift)
    sum_shift.step0()

    for copy in grad_halos:
        copy.wait()
    backward_out(gp, 0, fop, mix_p, cw, do, g_plain)
    sum_shift.step1()
    backward_attend(pr_p, es_p, rd_p, mix_p, do, dpr, 0, 2)
    sum_shift.step2()
    backward_attend(pr_p, es_p, rd_p, mix_p, do, dpr, 2, 4)
    sum_shift.step3()
    backward_weights(n_p, dpr, g_plain)
    sum_plain.step0()
    sum_shift.step4()
    backward_tokens(x, 0, fqp, cw, dpr, gf)
    ends.append(go(gf.at[:, :, :, away], gfo.at[own_rows], near))
    ends.append(keep(gf.at[:, :, :, lanes], gfo.at[own_rows]))
    sum_plain.step1()
    sum_shift.step5()
    sum_plain.step2()
    sum_shift.step6()
    sum_plain.step3()
    sum_plain.step4()
    sum_shift.step7()
    sum_plain.step5()
    sum_plain.step6()
    sum_plain.step7()
    sum_shift.wait()
    sum_plain.wait()
    for copy in ends:
        copy.wait()
    for copy, _ in qkv_p + out_p + qkv_s + out_s:
        copy.wait_send()
    for copy in shared + shared_out + shared_s + shared_out_s:
        copy.wait_send()


def shape(*dims, dtype=BF):
    return jax.ShapeDtypeStruct(dims, dtype)


GRID = (4, 4, 32, 512)
WIDE = (5, 5, 32, 512)
HELD = (8, 4, 32, 256)
SAVED = (
    ((4, 128, 512), BF),
    ((4, 128, 1536), BF),
    ((4, 4, 128, 512), BF),
    ((4, 128, 512), F32),
    ((4, 128, 512), BF),
)
SUM = (
    (2, 2, 4, 4, 2, 16, 256),
    (2, 2, 4, 4, 2, 16, 256),
    (2, 3, 2, 4, 2, 16, 256),
    (2, 2, 4, 2, 16, 256),
    (2, 3, 2, 2, 16, 256),
    (2, 2, 2, 16, 256),
    (3, 2, 16, 256),
)
SCRATCH = (
    [(s, BF) for s in (GRID, WIDE, WIDE, GRID, GRID, GRID, GRID, GRID)]
    + [((3, 512, 512), BF), ((512, 512), BF)] * 2
    + list(SAVED) * 2
    + [((4, 128, 512), BF), ((4, 128, 512), F32), ((4, 128, 1536), BF)]
    + [((2, 2, 2, 4, 4, 2, 16, 256), BF)] * 2
    + [(s, BF) for s in SUM] * 2
)


def cells(tokens):
    return tokens.reshape(8, 4, 4, 8, 256).transpose(0, 2, 1, 3, 4).reshape(8, 4, 32, 256)


def uncells(tokens):
    return tokens.reshape(8, 4, 4, 8, 256).transpose(0, 2, 1, 3, 4).reshape(32, 32, 256)


def on_device(fields, qkv_plain, out_plain, qkv_shift, out_shift, cotangent):
    factor = (fields.shape[0] * fields.shape[1] * 64) ** -0.5
    vmem = pl.BlockSpec(memory_space=pltpu.VMEM)
    hbm = pl.BlockSpec(memory_space=pl.ANY)
    f_shape = (2, 2, 4, 4, 2, 16, 256)
    result, grad_fields, f_plain, f_shift = pl.pallas_call(
        pair_kernel,
        out_shape=[shape(*HELD), shape(*HELD), shape(*f_shape), shape(*f_shape)],
        in_specs=[hbm] * 6,
        out_specs=[vmem] * 4,
        scratch_shapes=[pltpu.VMEM(s, t) for s, t in SCRATCH]
        + [
            pltpu.SemaphoreType.DMA((SENDS,)),
            pltpu.SemaphoreType.DMA((SENDS,)),
            pltpu.SemaphoreType.DMA((10,)),
        ],
        compiler_params=pltpu.CompilerParams(
            collective_id=0, has_side_effects=True, vmem_limit_bytes=VMEM_LIMIT
        ),
    )(
        cells(fields),
        cells(cotangent),
        qkv_plain.transpose(1, 0, 2),
        out_plain,
        qkv_shift.transpose(1, 0, 2),
        out_shift,
    )
    outs = []
    for summed in (f_plain, f_shift):
        summed = summed.reshape(2048, 256).astype(F32) * factor
        outs.append(summed[:1536].reshape(3, 512, 256).transpose(1, 0, 2))
        outs.append(jnp.concatenate([summed[1536:1792], summed[1792:]], 1))
    return (uncells(result), uncells(grad_fields), *outs)


def solution(mesh):
    in_specs = (
        P("lat", "lon", "mp"),
        P(None, None, "mp"),
        P("mp", None),
        P(None, None, "mp"),
        P("mp", None),
        P("lat", "lon", "mp"),
    )
    out_specs = (
        P("lat", "lon", "mp"),
        P("lat", "lon", "mp"),
        P(None, None, "mp"),
        P("mp", None),
        P(None, None, "mp"),
        P("mp", None),
    )
    return jax.shard_map(
        on_device, mesh=mesh, in_specs=in_specs, out_specs=out_specs, check_vma=False
    )
```

time: 176 us -> 117 us (0.66)
  Pallas kernels: 160 us -> 104 us
  other arithmetic: 5.65 us -> 2.34 us
    pallas_call x7 -> x1, Pallas kernels: 160 us -> 104 us  [on_device(): pl.pallas_call(pair_kernel, out_shape=[shape(*HELD), shape(*HELD), shape(...]
    another operation x1 -> x0, other arithmetic: 3.93 us -> none  [on_device(): g = jnp.stack([g_plain, g_shift]).reshape(2, 2, 2, 2, 4, 4, 2, 16, 256)]
    reshape x1 -> x2, local copies, waits for them, and re-layouts: 2.3 us -> 3.79 us  [cells(): tokens.reshape(8, 4, 4, 8, 256).transpose(0, 2, 1, 3, 4)]
where the time goes in v2:
time: 117 us
  Pallas kernels  104 us (89%)
  local copies, waits for them, and re-layouts  10.3 us (9%)
  other arithmetic  2.34 us (2%)
    pallas_call x1, Pallas kernels, on_device(): pl.pallas_call(pair_kernel, out_shape=[shape(*HELD), shape(*HELD), shape(...  104 us
    transpose x2, local copies, waits for them, and re-layouts, uncells(): tokens.reshape(8, 4, 4, 8, 256).transpose(0, 2, 1, 3, 4)  3.94 us
    reshape x2, local copies, waits for them, and re-layouts, cells(): tokens.reshape(8, 4, 4, 8, 256).transpose(0, 2, 1, 3, 4)  3.79 us
    slice x2, local copies, waits for them, and re-layouts, on_device(): outs.append(summed[:1536].reshape(3, 512, 256).transpose(1, 0, 2))  2.49 us

profile of v2, /device:TPU:1, one launch (start us, length us, event | category | flops | bytes accessed | tf_op | source)
XLA Modules:
  0.0 117.0 jit_solution(8797696000322437421)
XLA Ops:
  0.6 1.9 %copy.19 = bf16[8,4,4,8,256]{4,3,1,2,0:T(8,128)(2,1)} copy(bf16[8,4,4,8,256]{4,3,2,1,0:T(8,128)(2,1)} %bitcast.40) | data formatting | bytes 1048576 | tf_op jit(solution)/shard_map/reshape | solution.py:555
  2.5 1.9 %copy.18 = bf16[8,4,4,8,256]{4,3,1,2,0:T(8,128)(2,1)} copy(bf16[8,4,4,8,256]{4,3,2,1,0:T(8,128)(2,1)} %bitcast.41) | data formatting | bytes 1048576 | tf_op jit(solution)/shard_map/reshape | solution.py:555
  4.4 103.6 %shard_map.109 = (bf16[8,4,32,256]{3,2,1,0:T(8,128)(2,1)}, bf16[8,4,32,256]{3,2,1,0:T(8,128)(2,1)}, bf16[2,2,4,4,2,16,256]{6,5,4,3,2,1,0:T(8,128)(2,1)}, bf16[2,2,4,4,2,16,256]{6,5,4,3,2,1,0:T(8,128)(2,1)}) custom-call(bf16[8,4,32,256]{3,2,1,0:T(8,128)(2,1)} %bitcast.34, bf16[8,4,32,256]{3,2,1,0:T(8,128)(2,1)} %bitcast.35, bf16[3,512,256]{2,1,0:T(8,128)(2,1)} %bitcast.38, ...), custom_call_target="tpu_custom_call" | custom-call | tf_op jit(solution)/shard_map/pallas_call | solution.py:567
  108.1 0.0 copy-start
  108.1 0.0 copy-start.1
  108.1 2.0 %copy.14 = bf16[8,4,4,8,256]{4,3,2,1,0:T(8,128)(2,1)} copy(bf16[8,4,4,8,256]{4,3,1,2,0:T(8,128)(2,1)} %bitcast.45) | data formatting | bytes 1048576 | tf_op jit(solution)/shard_map/transpose | solution.py:559
  110.1 1.9 %copy.15 = bf16[8,4,4,8,256]{4,3,2,1,0:T(8,128)(2,1)} copy(bf16[8,4,4,8,256]{4,3,1,2,0:T(8,128)(2,1)} %bitcast.44) | data formatting | bytes 1048576 | tf_op jit(solution)/shard_map/transpose | solution.py:559
  112.0 0.0 copy-done
  112.0 0.0 copy-done.1
  112.0 0.6 convert_multiply_fusion
  112.7 1.2 %slice.24 = f32[1536,256]{1,0:T(8,128)} slice(f32[2048,256]{1,0:T(8,128)S(1)} %bitcast.33), slice={[0:1536], [0:256]} | slice | bytes 3145728 | tf_op jit(solution)/shard_map/slice | solution.py:592
  113.9 0.9 pad_maximum_fusion
  114.8 1.2 %slice.27 = f32[1536,256]{1,0:T(8,128)} slice(f32[2048,256]{1,0:T(8,128)S(1)} %bitcast.31), slice={[0:1536], [0:256]} | slice | bytes 3145728 | tf_op jit(solution)/shard_map/slice | solution.py:592
  116.1 0.9 pad_maximum_fusion.1
  (2 shorter events, 0.1 us)
Async XLA Ops:
  108.1 4.0 %copy-start = (bf16[2,2,4,4,2,16,256]{6,5,4,3,2,1,0:T(8,128)(2,1)S(1)}, bf16[2,2,4,4,2,16,256]{6,5,4,3,2,1,0:T(8,128)(2,1)}, u32[]{:S(2)}) copy-start(bf16[2,2,4,4,2,16,256]{6,5,4,3,2,1,0:T(8,128)(2,1)} %get-tuple-element.12) | copy-start | bytes 3145732
  108.1 4.0 %copy-start.1 = (bf16[2,2,4,4,2,16,256]{6,5,4,3,2,1,0:T(8,128)(2,1)S(1)}, bf16[2,2,4,4,2,16,256]{6,5,4,3,2,1,0:T(8,128)(2,1)}, u32[]{:S(2)}) copy-start(bf16[2,2,4,4,2,16,256]{6,5,4,3,2,1,0:T(8,128)(2,1)} %get-tuple-element.13) | copy-start | bytes 3145732

commit v3 on v2

--- a/solution.py
+++ b/solution.py
@@ -95,17 +95,36 @@
     ref[pl.ds(2 * i, 2), pl.ds(2 * j, 2)] = value.reshape(2, 2, 32, D)
 
 
-def forward_norm(x, offset, n, low, high):
+def rows_window(ref, w):
+    i, j = w // 2, lax.rem(w, 2)
+    got = ref[pl.ds(8 * i, 8), pl.ds(pl.multiple_of(16 * j, 16), 16)]
+    return got.reshape(128, D)
+
+
+def put_rows(ref, w, value):
+    i, j = w // 2, lax.rem(w, 2)
+    ref[pl.ds(8 * i, 8), pl.ds(pl.multiple_of(16 * j, 16), 16)] = value.reshape(8, 16, D)
+
+
+def cells_of(value):
+    return value.reshape(2, 4, 2, 8, D).transpose(0, 2, 1, 3, 4).reshape(128, D)
+
+
+def rows_of(value):
+    return value.reshape(2, 2, 4, 8, D).transpose(0, 2, 1, 3, 4).reshape(128, D)
+
+
+def forward_norm(take, n, low, high):
     def norm(w, carry):
-        n[w] = standardize(window(x, w, offset).astype(F32))[0].astype(BF)
+        n[w] = standardize(take(w).astype(F32))[0].astype(BF)
         return carry
 
     lax.fori_loop(low, high, norm, 0)
 
 
-def forward_project(n, wq, pr, low, high):
+def forward_project(n, wq, pr, low, high, kinds=(0, 1, 2)):
     count = high - low
-    for c in range(3):
+    for c in kinds:
         for j in range(2):
             cols = slice(c * 512 + j * 256, c * 512 + (j + 1) * 256)
             got = dot(n[low:high].reshape(count * 128, 512), wq[c, :, j * 256 : (j + 1) * 256])
@@ -139,25 +158,31 @@
     lax.fori_loop(low, high, attend, 0)
 
 
-def forward_out(x, offset, wo, mix, out, low, high):
+def forward_out(take, wo, mix, put, work):
+    work[...] = dot(mix[...].reshape(512, 512), wo[...]).reshape(4, 128, 512)
+
     def project(w, carry):
-        value = window(x, w, offset).astype(F32) + dot(mix[w], wo[...])
-        put_window(out, w, value.astype(BF))
+        put(w, take(w).astype(F32) + work[w])
         return carry
 
-    lax.fori_loop(low, high, project, 0)
-
-
-def backward_out(ct, ct_offset, wo, mix, cw, do, g):
+    lax.fori_loop(0, 4, project, 0)
+
+
+def backward_do(take, wo, cw, do, low, high):
+    count = high - low
+
     def gather(w, carry):
-        cw[w] = window(ct, w, ct_offset)
+        cw[w] = take(w)
         return carry
 
-    lax.fori_loop(0, 4, gather, 0)
+    lax.fori_loop(low, high, gather, 0)
     for j in range(2):
         cols = slice(j * 256, (j + 1) * 256)
-        got = dot(cw[...].reshape(512, 512), wo[cols, :], NT)
-        do[:, :, cols] = got.reshape(4, 128, 256)
+        got = dot(cw[low:high].reshape(count * 128, 512), wo[cols, :], NT)
+        do[low:high, :, cols] = got.reshape(count, 128, 256)
+
+
+def backward_out(mix, cw, g):
     for j in range(2):
         cols = slice(j * 256, (j + 1) * 256)
         got = dot(mix[:, :, cols].reshape(512, 256), cw[...].reshape(512, 512), TN).astype(BF)
@@ -200,21 +225,26 @@
             g[j, c // 2, c % 2] = got.astype(BF).reshape(4, 4, 2, 16, 256)
 
 
-def backward_tokens(x, offset, wq, cw, dpr, out):
+def backward_tokens(take, wq, cw, dpr, put, work, low, high):
+    count = high - low
+    grad = dot(dpr[low:high, :, 0:512].reshape(count * 128, 512), wq[0], NT)
+    for c in (1, 2):
+        part = dpr[low:high, :, c * 512 : (c + 1) * 512].reshape(count * 128, 512)
+        grad = grad + dot(part, wq[c], NT)
+    work[low:high] = grad.reshape(count, 128, 512)
+
     def finish(w, carry):
-        grad = dot(dpr[w, :, 0:512], wq[0], NT)
-        grad = grad + dot(dpr[w, :, 512:1024], wq[1], NT)
-        grad = grad + dot(dpr[w, :, 1024:1536], wq[2], NT)
-        standard, inv = standardize(window(x, w, offset).astype(F32))
+        grad = work[w]
+        standard, inv = standardize(take(w).astype(F32))
         back = inv * (
             grad
             - jnp.mean(grad, -1, keepdims=True)
             - standard * jnp.mean(grad * standard, -1, keepdims=True)
         )
-        put_window(out, w, (cw[w].astype(F32) + back).astype(BF))
+        put(w, cw[w].astype(F32) + back)
         return carry
 
-    lax.fori_loop(0, 4, finish, 0)
+    lax.fori_loop(low, high, finish, 0)
 
 
 class Sum:
@@ -288,48 +318,51 @@
 
     def step3(self):
         self.wait()
-        a1, r2, a2, r3, mp, x_hi = self.a1, self.r2, self.a2, self.r3, self.mp, self.x_hi
+        a1, r2, a2, r3, mp = self.a1, self.r2, self.a2, self.r3, self.mp
         for part, (ia, along_a, ib, along_b) in enumerate(self.ways):
             total = a1[:, part, ib].astype(F32)
             for k in range(3):
                 total = total + r2[part, k].astype(F32)
             a2[:, part] = total.astype(BF)
         self.flying = [
-            self.go(a2.at[1 - mp, :, x_hi], r3.at[0], self.near),
-            self.go(a2.at[1 - mp, :, 1 - x_hi], r3.at[1], self.far),
-            self.go(a2.at[mp, :, 1 - x_hi], r3.at[2], self.opposite),
+            self.go(a2.at[1 - mp], r3.at[0], self.near),
+            self.go(a2.at[1 - mp], r3.at[1], self.far),
+            self.go(a2.at[mp], r3.at[2], self.opposite),
         ]
 
     def step4(self):
         self.wait()
-        total = self.a2[self.mp, :, self.x_hi].astype(F32)
-        for k in range(3):
-            total = total + self.r3[k].astype(F32)
-        total = total.astype(BF)
+        same = self.a2[self.mp].astype(F32) + self.r3[2].astype(F32)
+        other = self.r3[0].astype(F32) + self.r3[1].astype(F32)
+        total = (same + other).astype(BF)
         for part, (ia, along_a, ib, along_b) in enumerate(self.ways):
-            self.f[self.core, part, ia, ib, self.x_hi] = total[part]
-        for part, (ia, along_a, ib, along_b) in enumerate(self.ways):
-            spot = self.f.at[self.core, part, ia, ib, self.x_hi]
-            self.flying.append(self.go(spot, spot, self.opposite))
-
-    def step5(self):
-        self.wait()
+            self.f[self.core, part, ia, ib] = total[part]
         for step in (1, 2, 3):
             for part, (ia, along_a, ib, along_b) in enumerate(self.ways):
                 spot = self.f.at[self.core, part, ia, ib]
                 self.flying.append(self.go(spot, spot, along_b(step)))
 
-    def step6(self):
+    def step5(self):
         self.wait()
+        self.coming = []
         for step in (1, 2, 3):
             for part, (ia, along_a, ib, along_b) in enumerate(self.ways):
                 spot = self.f.at[self.core, part, ia]
-                self.flying.append(self.go(spot, spot, along_a(step)))
-
-    def step7(self):
+                arrives = self.f.at[self.core, part, lax.rem(ia + 4 - step, 4)]
+                self.coming.append((self.go(spot, spot, along_a(step)), arrives))
+        for part, (ia, along_a, ib, along_b) in enumerate(self.ways):
+            spot = self.f.at[self.core, part, ia]
+            self.flying.append(self.go(spot, spot, self.sibling))
+
+    def step6(self):
+        for copy, spot in self.coming:
+            copy.wait_recv()
+            self.flying.append(self.go(spot, spot, self.sibling))
+
+    def last(self):
         self.wait()
-        spot = self.f.at[self.core]
-        self.flying = [self.go(spot, spot, self.sibling)]
+        for copy, _ in self.coming:
+            copy.wait_send()
 
 
 def around(lat, lon, mp, step):
@@ -339,17 +372,16 @@
 
 
 SENDS = 112
-NEAR_ROWS = (96, 256)
 
 
 def pair_kernel(
     fc, cc, wqp, wop, wqs, wos,
     ro, gfo, f_plain, f_shift,
-    x, hx, cx, rs, rp, gs, gp, gf,
+    x, hx, cx, rs, rp, gs, gp, gf, rn,
     fqp, fop, fqs, fos,
     n_p, pr_p, es_p, rd_p, mix_p,
     n_s, pr_s, es_s, rd_s, mix_s,
-    cw, do, dpr,
+    cw, do, dpr, cn,
     g_plain, g_shift,
     *rest,
 ):
@@ -367,8 +399,8 @@
     )
     lanes = pl.ds(pl.multiple_of(mp * 256, 256), 256)
     away = pl.ds(pl.multiple_of((1 - mp) * 256, 256), 256)
-    other_rows = pl.ds((1 - mp) * 4, 4)
-    own_rows = pl.ds(mp * 4, 4)
+    other_rows = pl.ds((1 - mp) * 16, 16)
+    own_rows = pl.ds(mp * 16, 16)
     own = pl.ds(0, 4)
     kept = []
 
@@ -378,86 +410,129 @@
         kept.append(copy)
         return copy
 
-    def weight(src, dst, split):
-        parts = []
-        for k, (base, size) in enumerate(((0, split // 2), (split, (512 - split) // 2))):
-            rows = pl.ds(pl.multiple_of(base + core * size, 16), size)
-            copy = go(src.at[:, rows], dst.at[:, rows, lanes], (near, far)[k])
-            parts.append((copy, dst.at[:, rows, away]))
-        return parts
-
-    def weight_out(src, dst):
+    def weight(src, dst, c, peer):
+        rows = pl.ds(pl.multiple_of(core * 256, 256), 256)
+        return go(src.at[c, rows], dst.at[c, rows, lanes], peer), dst.at[c, rows, away]
+
+    def weight_out(src, dst, peer):
         rows = pl.ds(pl.multiple_of(core * 128, 128), 128)
         there = pl.ds(pl.multiple_of(mp * 256 + core * 128, 128), 128)
         here = pl.ds(pl.multiple_of((1 - mp) * 256 + core * 128, 128), 128)
-        return [(go(src.at[rows], dst.at[there], far), dst.at[here])]
-
-    def pass_on(parts):
-        shared = []
-        for copy, spot in parts:
-            copy.wait_recv()
-            shared.append(go(spot, spot, sibling))
-        return shared
-
-    fields_copy = go(fc.at[other_rows], x.at[:, :, :, lanes], near)
-    qkv_p = weight(wqp, fqp, NEAR_ROWS[0])
-    out_p = weight_out(wop, fop)
-    cot_copy = go(cc.at[other_rows], cx.at[own, own, :, lanes], near)
-    qkv_s = weight(wqs, fqs, NEAR_ROWS[1])
-    out_s = weight_out(wos, fos)
+        return go(src.at[rows], dst.at[there], peer), dst.at[here]
+
+    y, z = lax.rem(lat, 4), lon // 2
+    along_y, along_z = sum_plain.ways[0][1], sum_plain.ways[0][3]
+    rows_s = pl.ds(pl.multiple_of(core * 256 + y * 64, 64), 64)
+    half_s = pl.ds(pl.multiple_of(core * 256, 256), 256)
+    at_o = core * 128 + z * 32
+    rows_o = pl.ds(pl.multiple_of(at_o, 32), 32)
+    there_o = pl.ds(pl.multiple_of(mp * 256 + at_o, 32), 32)
+    here_o = pl.ds(pl.multiple_of((1 - mp) * 256 + at_o, 32), 32)
+    half_o = pl.ds(pl.multiple_of((1 - mp) * 256 + core * 128, 128), 128)
+
+    unsent = []
+
+    def pass_on(part):
+        copy, spot = part
+        copy.wait_recv()
+        unsent.append(copy)
+        passed = go(spot, spot, sibling)
+        unsent.append(passed)
+        return passed
+
+    fields_copy = go(fc.at[other_rows], x.at[:, :, lanes], near)
+    qkv_p = [weight(wqp, fqp, c, far) for c in range(3)]
+    x_kept = keep(fc.at[own_rows], x.at[:, :, lanes])
     mp_rows = pl.ds(pl.multiple_of(mp * 256, 256), 256)
-    x_kept = keep(fc.at[own_rows], x.at[:, :, :, lanes])
-    wq_kept = keep(wqp, fqp.at[:, :, lanes])
     others = [
+        keep(wqp, fqp.at[:, :, lanes]),
         keep(wop, fop.at[mp_rows]),
-        keep(cc.at[own_rows], cx.at[own, own, :, lanes]),
         keep(wqs, fqs.at[:, :, lanes]),
         keep(wos, fos.at[mp_rows]),
+        keep(cc.at[own_rows], cn.at[:, :, lanes]),
     ]
+
+    def take_x(w):
+        return rows_window(x, w)
+
+    def put_hidden(w, value):
+        put_window(hx, w, cells_of(value).astype(BF))
 
     fields_copy.wait()
     x_kept.wait()
-    forward_norm(x, 0, n_p, 0, 4)
-    shared = pass_on(qkv_p)
-    wq_kept.wait()
-    for copy in shared:
-        copy.wait_recv()
-    forward_project(n_p, fqp, pr_p, 0, 4)
-    shared_out = pass_on(out_p)
-    forward_attend(pr_p, es_p, rd_p, mix_p, None, 0, 4)
+    over_x = [
+        go(wqs.at[:, rows_s], fqs.at[:, rows_s, lanes], near),
+        go(wos.at[rows_o], fos.at[there_o], near),
+    ]
+    forward_norm(take_x, n_p, 0, 4)
     for copy in others:
         copy.wait()
-    for copy in shared_out:
+    passed = pass_on(qkv_p[0])
+    for c in range(3):
+        passed_next = pass_on(qkv_p[c + 1]) if c < 2 else None
+        passed.wait_recv()
+        if c == 2:
+            out_p = weight_out(wop, fop, far)
+        forward_project(n_p, fqp, pr_p, 0, 4, (c,))
+        passed = passed_next
+    for copy in over_x:
         copy.wait_recv()
-    forward_out(x, 0, fop, mix_p, hx, 0, 4)
+    unsent.extend(over_x)
+    spread = []
+    for step in (1, 2, 3):
+        spot = fqs.at[:, rows_s, away]
+        spread.append(go(spot, spot, along_y(step)))
+        spot = fos.at[here_o]
+        spread.append(go(spot, spot, along_z(step)))
+    cot_copy = go(cc.at[other_rows], cn.at[:, :, lanes], near)
+    forward_attend(pr_p, es_p, rd_p, mix_p, None, 0, 4)
+    pass_on(out_p).wait_recv()
+    forward_out(take_x, fop, mix_p, put_hidden, do)
 
     halos = [
         go(hx.at[0, own], hx.at[4, own], row_prev),
         go(hx.at[own, 0], hx.at[own, 4], col_prev),
         go(hx.at[0, 0], hx.at[4, 4], corner_prev),
     ]
+
+    def take_hidden(w):
+        return window(hx, w, 1)
+
+    for copy in spread:
+        copy.wait()
+    spot = fqs.at[:, half_s, away]
+    passed_qkv = go(spot, spot, sibling)
+    spot = fos.at[half_o]
+    passed_out = go(spot, spot, sibling)
+    forward_norm(take_hidden, n_s, 0, 1)
+    passed_qkv.wait()
+    forward_project(n_s, fqs, pr_s, 0, 1)
+    cut = (lat * 2 + mp) == 15
+    forward_attend(pr_s, es_s, rd_s, mix_s, cut, 0, 1)
+
     cot_copy.wait()
+
+    def into_cells(w, carry):
+        put_window(cx, w, cells_of(rows_window(cn, w).astype(F32)).astype(BF))
+        return carry
+
+    lax.fori_loop(0, 4, into_cells, 0)
+    for copy in halos:
+        copy.wait()
     cot_halos = [
         go(cx.at[0, own], cx.at[4, own], row_prev),
         go(cx.at[own, 0], cx.at[own, 4], col_prev),
         go(cx.at[0, 0], cx.at[4, 4], corner_prev),
     ]
-    shared_s = pass_on(qkv_s)
-    forward_norm(hx, 1, n_s, 0, 1)
-    for copy in shared_s:
-        copy.wait_recv()
-    cut = (lat * 2 + mp) == 15
-    forward_project(n_s, fqs, pr_s, 0, 1)
-    shared_out_s = pass_on(out_s)
-    forward_attend(pr_s, es_s, rd_s, mix_s, cut, 0, 1)
-    for copy in halos:
-        copy.wait()
-    forward_norm(hx, 1, n_s, 1, 4)
+    forward_norm(take_hidden, n_s, 1, 4)
     forward_project(n_s, fqs, pr_s, 1, 4)
     forward_attend(pr_s, es_s, rd_s, mix_s, cut, 1, 4)
-    for copy in shared_out_s:
-        copy.wait_recv()
-    forward_out(hx, 1, fos, mix_s, rs, 0, 4)
+    passed_out.wait()
+
+    def put_result(w, value):
+        put_window(rs, w, value.astype(BF))
+
+    forward_out(take_hidden, fos, mix_s, put_result, do)
 
     low, high = pl.ds(0, 3), pl.ds(1, 3)
 
@@ -471,51 +546,105 @@
 
     result_halos = narrow(rs, rp)
 
+    def take_cot(w):
+        return window(cx, w, 1)
+
+    def put_grad(w, value):
+        put_window(gs, w, value.astype(BF))
+
     for copy in cot_halos:
         copy.wait()
-    backward_out(cx, 1, fos, mix_s, cw, do, g_shift)
+    backward_do(take_cot, fos, cw, do, 0, 4)
+    backward_out(mix_s, cw, g_shift)
     backward_attend(pr_s, es_s, rd_s, mix_s, do, dpr, 0, 4)
-    backward_tokens(hx, 1, fqs, cw, dpr, gs)
+    backward_tokens(take_hidden, fqs, cw, dpr, put_grad, do, 0, 4)
     grad_halos = narrow(gs, gp)
+    backward_weights(n_s, dpr, g_shift)
+    sum_shift.step0()
     for copy in result_halos:
         copy.wait()
-    ends = [go(rp.at[:, :, :, away], ro.at[own_rows], near)]
-    ends.append(keep(rp.at[:, :, :, lanes], ro.at[own_rows]))
-    backward_weights(n_s, dpr, g_shift)
-    sum_shift.step0()
-
+
+    def into_rows(w, carry):
+        put_rows(rn, w, rows_of(window(rp, w, 0).astype(F32)).astype(BF))
+        return carry
+
+    lax.fori_loop(0, 4, into_rows, 0)
+    ends = [go(rn.at[:, :, away], ro.at[own_rows], near)]
+    ends.append(keep(rn.at[:, :, lanes], ro.at[own_rows]))
+
+    def take_back(w):
+        return rows_of(window(gp, w, 0).astype(F32)).astype(BF)
+
+    def put_fields(w, value):
+        put_rows(gf, w, value.astype(BF))
+
+    grad_halos.pop().wait()
+    backward_do(take_back, fop, cw, do, 3, 4)
+    backward_attend(pr_p, es_p, rd_p, mix_p, do, dpr, 3, 4)
     for copy in grad_halos:
         copy.wait()
-    backward_out(gp, 0, fop, mix_p, cw, do, g_plain)
+    backward_do(take_back, fop, cw, do, 0, 3)
+    backward_out(mix_p, cw, g_plain)
     sum_shift.step1()
-    backward_attend(pr_p, es_p, rd_p, mix_p, do, dpr, 0, 2)
+    backward_attend(pr_p, es_p, rd_p, mix_p, do, dpr, 0, 3)
     sum_shift.step2()
-    backward_attend(pr_p, es_p, rd_p, mix_p, do, dpr, 2, 4)
-    sum_shift.step3()
     backward_weights(n_p, dpr, g_plain)
     sum_plain.step0()
+    for half in range(2):
+        backward_tokens(take_x, fqp, cw, dpr, put_fields, do, half * 2, half * 2 + 2)
+        rows = pl.ds(half * 8, 8)
+        there = pl.ds(mp * 16 + half * 8, 8)
+        ends.append(go(gf.at[rows, :, away], gfo.at[there], near))
+        ends.append(keep(gf.at[rows, :, lanes], gfo.at[there]))
+        if half == 0:
+            sum_plain.step1()
+            sum_shift.step3()
     sum_shift.step4()
-    backward_tokens(x, 0, fqp, cw, dpr, gf)
-    ends.append(go(gf.at[:, :, :, away], gfo.at[own_rows], near))
-    ends.append(keep(gf.at[:, :, :, lanes], gfo.at[own_rows]))
-    sum_plain.step1()
+    sum_plain.step2()
     sum_shift.step5()
-    sum_plain.step2()
+    sum_plain.step3()
     sum_shift.step6()
-    sum_plain.step3()
     sum_plain.step4()
-    sum_shift.step7()
     sum_plain.step5()
     sum_plain.step6()
-    sum_plain.step7()
-    sum_shift.wait()
-    sum_plain.wait()
+    sum_shift.last()
+    sum_plain.last()
     for copy in ends:
         copy.wait()
-    for copy, _ in qkv_p + out_p + qkv_s + out_s:
+    for copy in unsent:
         copy.wait_send()
-    for copy in shared + shared_out + shared_s + shared_out_s:
-        copy.wait_send()
+
+
+def last_kernel(
+    factor, f_plain, f_shift, r, gf, qkv_p, out_p, qkv_s, out_s, ro, gfo, raw, wide, held, came, gone
+):
+    coming, going = [], []
+
+    def move(src, dst, sem, to):
+        copy = pltpu.make_async_copy(src, dst, sem)
+        copy.start()
+        to.append(copy)
+
+    for n in range(8):
+        rows = pl.ds(n % 4 * 512, 512)
+        move((f_plain, f_shift)[n // 4].at[rows], raw.at[n], came.at[n], coming)
+    for n, src in enumerate((r, gf)):
+        move(src, held.at[n], came.at[8 + n], coming)
+    for n in range(8):
+        coming[n].wait()
+        wide[n] = raw[n].astype(F32) * factor
+        if n % 4 < 3:
+            move(wide.at[n], (qkv_p, qkv_s)[n // 4].at[n % 4], gone.at[n], going)
+        else:
+            for k in range(2):
+                cols = pl.ds(k * 256, 256)
+                dst = (out_p, out_s)[n // 4].at[:, cols]
+                move(wide.at[n, cols], dst, gone.at[8 + n // 4 * 2 + k], going)
+    for n, dst in enumerate((ro, gfo)):
+        coming[8 + n].wait()
+        move(held.at[n], dst, gone.at[12 + n], going)
+    for copy in going:
+        copy.wait()
 
 
 def shape(*dims, dtype=BF):
@@ -524,7 +653,8 @@
 
 GRID = (4, 4, 32, 512)
 WIDE = (5, 5, 32, 512)
-HELD = (8, 4, 32, 256)
+ROWS = (16, 32, 512)
+HELD = (32, 32, 256)
 SAVED = (
     ((4, 128, 512), BF),
     ((4, 128, 1536), BF),
@@ -539,24 +669,16 @@
     (2, 2, 4, 2, 16, 256),
     (2, 3, 2, 2, 16, 256),
     (2, 2, 2, 16, 256),
-    (3, 2, 16, 256),
+    (3, 2, 2, 16, 256),
 )
 SCRATCH = (
-    [(s, BF) for s in (GRID, WIDE, WIDE, GRID, GRID, GRID, GRID, GRID)]
+    [(s, BF) for s in (ROWS, WIDE, WIDE, GRID, GRID, GRID, GRID, ROWS, ROWS)]
     + [((3, 512, 512), BF), ((512, 512), BF)] * 2
     + list(SAVED) * 2
-    + [((4, 128, 512), BF), ((4, 128, 512), F32), ((4, 128, 1536), BF)]
+    + [((4, 128, 512), BF), ((4, 128, 512), F32), ((4, 128, 1536), BF), (ROWS, BF)]
     + [((2, 2, 2, 4, 4, 2, 16, 256), BF)] * 2
     + [(s, BF) for s in SUM] * 2
 )
-
-
-def cells(tokens):
-    return tokens.reshape(8, 4, 4, 8, 256).transpose(0, 2, 1, 3, 4).reshape(8, 4, 32, 256)
-
-
-def uncells(tokens):
-    return tokens.reshape(8, 4, 4, 8, 256).transpose(0, 2, 1, 3, 4).reshape(32, 32, 256)
 
 
 def on_device(fields, qkv_plain, out_plain, qkv_shift, out_shift, cotangent):
@@ -573,25 +695,42 @@
         + [
             pltpu.SemaphoreType.DMA((SENDS,)),
             pltpu.SemaphoreType.DMA((SENDS,)),
-            pltpu.SemaphoreType.DMA((10,)),
+            pltpu.SemaphoreType.DMA((12,)),
         ],
         compiler_params=pltpu.CompilerParams(
             collective_id=0, has_side_effects=True, vmem_limit_bytes=VMEM_LIMIT
         ),
     )(
-        cells(fields),
-        cells(cotangent),
+        fields,
+        cotangent,
         qkv_plain.transpose(1, 0, 2),
         out_plain,
         qkv_shift.transpose(1, 0, 2),
         out_shift,
     )
-    outs = []
-    for summed in (f_plain, f_shift):
-        summed = summed.reshape(2048, 256).astype(F32) * factor
-        outs.append(summed[:1536].reshape(3, 512, 256).transpose(1, 0, 2))
-        outs.append(jnp.concatenate([summed[1536:1792], summed[1792:]], 1))
-    return (uncells(result), uncells(grad_fields), *outs)
+    qkv, out = shape(3, 512, 256, dtype=F32), shape(256, 512, dtype=F32)
+    qkv_p, out_p, qkv_s, out_s, result, grad_fields = pl.pallas_call(
+        functools.partial(last_kernel, factor),
+        out_shape=[qkv, out, qkv, out, shape(*HELD), shape(*HELD)],
+        in_specs=[hbm] * 4,
+        out_specs=[hbm] * 6,
+        scratch_shapes=[
+            pltpu.VMEM((8, 512, 256), BF),
+            pltpu.VMEM((8, 512, 256), F32),
+            pltpu.VMEM((2,) + HELD, BF),
+            pltpu.SemaphoreType.DMA((10,)),
+            pltpu.SemaphoreType.DMA((14,)),
+        ],
+        compiler_params=pltpu.CompilerParams(vmem_limit_bytes=VMEM_LIMIT),
+    )(f_plain.reshape(2048, 256), f_shift.reshape(2048, 256), result, grad_fields)
+    return (
+        result,
+        grad_fields,
+        qkv_p.transpose(1, 0, 2),
+        out_p,
+        qkv_s.transpose(1, 0, 2),
+        out_s,
+    )
 
 
 def solution(mesh):

time: 117 us -> 103 us (0.88)
  local copies, waits for them, and re-layouts: 10.3 us -> 0 us
  other arithmetic: 2.34 us -> 0 us
  Pallas kernels: 104 us -> 102 us
    pallas_call x1, Pallas kernels: 104 us -> 98.9 us  [on_device(): pl.pallas_call(pair_kernel, out_shape=[shape(*HELD), shape(*HELD), shape(...]
    transpose x2 -> x0, local copies, waits for them, and re-layouts: 3.94 us -> none  [uncells(): tokens.reshape(8, 4, 4, 8, 256).transpose(0, 2, 1, 3, 4)]
    reshape x2 -> x0, local copies, waits for them, and re-layouts: 3.79 us -> none  [cells(): tokens.reshape(8, 4, 4, 8, 256).transpose(0, 2, 1, 3, 4)]
    pallas_call x0 -> x1, Pallas kernels: none -> 3.53 us  [on_device(): pl.pallas_call(functools.partial(last_kernel, factor), out_shape=[qkv, ou...]
    slice x4 -> x0, local copies, waits for them, and re-layouts: 2.56 us -> none  [the longest x2 2.49 us: on_device(): outs.append(summed[:1536].reshape(3, 512, 256).transpose(1, 0, 2))]
    concatenate x2 -> x0, other arithmetic: 1.73 us -> none  [on_device(): outs.append(jnp.concatenate([summed[1536:1792], summed[1792:]], 1))]
where the time goes in v3:
time: 103 us
  Pallas kernels  102 us (99%)
    pallas_call x1, Pallas kernels, on_device(): pl.pallas_call(pair_kernel, out_shape=[shape(*HELD), shape(*HELD), shape(...  98.9 us
    pallas_call x1, Pallas kernels, on_device(): pl.pallas_call(functools.partial(last_kernel, factor), out_shape=[qkv, ou...  3.53 us

profile of v3, /device:TPU:1, one launch (start us, length us, event | category | flops | bytes accessed | tf_op | source)
XLA Modules:
  0.0 103.1 jit_solution(15841624808254955530)
XLA Ops:
  0.6 98.9 %shard_map.109 = (bf16[32,32,256]{2,1,0:T(8,128)(2,1)}, bf16[32,32,256]{2,1,0:T(8,128)(2,1)}, bf16[2,2,4,4,2,16,256]{6,5,4,3,2,1,0:T(8,128)(2,1)}, bf16[2,2,4,4,2,16,256]{6,5,4,3,2,1,0:T(8,128)(2,1)}) custom-call(bf16[32,32,256]{2,1,0:T(8,128)(2,1)} %fc.1, bf16[32,32,256]{2,1,0:T(8,128)(2,1)} %cc.1, bf16[3,512,256]{2,1,0:T(8,128)(2,1)} %bitcast.8, ...), custom_call_target="tpu_custom_call" | custom-call | tf_op jit(solution)/shard_map/pallas_call | solution.py:689
  99.6 3.5 %shard_map.110 = (f32[3,512,256]{2,1,0:T(8,128)}, f32[256,512]{1,0:T(8,128)}, f32[3,512,256]{2,1,0:T(8,128)}, f32[256,512]{1,0:T(8,128)}, bf16[32,32,256]{2,1,0:T(8,128)(2,1)}, /*index=5*/bf16[32,32,256]{2,1,0:T(8,128)(2,1)}) custom-call(bf16[2048,256]{1,0:T(8,128)(2,1)} %bitcast.6, bf16[2048,256]{1,0:T(8,128)(2,1)} %bitcast.7, ...), custom_call_target="tpu_custom_call" | custom-call | tf_op jit(solution)/shard_map/pallas_call | solution.py:712

commit v4 on v3

--- a/solution.py
+++ b/solution.py
@@ -122,16 +122,22 @@
     lax.fori_loop(low, high, norm, 0)
 
 
-def forward_project(n, wq, pr, low, high, kinds=(0, 1, 2)):
+def lanes_at(start, size):
+    if isinstance(start, int):
+        return slice(start, start + size)
+    return pl.ds(pl.multiple_of(start, size), size)
+
+
+def forward_project(n, wq, pr, low, high, groups=(0, 1)):
     count = high - low
-    for c in kinds:
-        for j in range(2):
-            cols = slice(c * 512 + j * 256, c * 512 + (j + 1) * 256)
-            got = dot(n[low:high].reshape(count * 128, 512), wq[c, :, j * 256 : (j + 1) * 256])
-            pr[low:high, :, cols] = got.astype(BF).reshape(count, 128, 256)
-
-
-def forward_attend(pr, es, rd, mix, cut, low, high):
+    for j in groups:
+        for c in range(3):
+            weight = wq[c, :, lanes_at(j * 256, 256)]
+            got = dot(n[low:high].reshape(count * 128, 512), weight)
+            pr[low:high, :, lanes_at(c * 512 + j * 256, 256)] = got.astype(BF).reshape(count, 128, 256)
+
+
+def forward_attend(pr, es, rd, mix, cut, low, high, chosen=(0, 1, 2, 3)):
     masks = head_masks()
     ones = spread_heads(jnp.ones((128, 128), BF), masks)
     if cut is not None:
@@ -140,32 +146,41 @@
         same = q_half == k_half
 
     def attend(w, carry):
-        for s in range(4):
-            q = pr[w, :, s * 128 : (s + 1) * 128]
-            k = spread_heads(pr[w, :, 512 + s * 128 : 512 + (s + 1) * 128], masks)
-            v = spread_heads(pr[w, :, 1024 + s * 128 : 1024 + (s + 1) * 128], masks)
-            e = jnp.exp2(dot(q, k, NT) * (SCALE * LOG2E))
+        scores = []
+        for s in chosen:
+            q = pr[w, :, lanes_at(s * 128, 128)]
+            k = spread_heads(pr[w, :, lanes_at(512 + s * 128, 128)], masks)
+            scores.append(dot(q, k, NT))
+        es_now = []
+        for score in scores:
+            e = jnp.exp2(score * (SCALE * LOG2E))
             if cut is not None:
                 e = jnp.where(same | jnp.logical_not(cut & (w >= 2)), e, 0.0)
-            e = e.astype(BF)
+            es_now.append(e.astype(BF))
+        both = []
+        for s, e in zip(chosen, es_now):
+            v = spread_heads(pr[w, :, lanes_at(1024 + s * 128, 128)], masks)
+            both.append(dot(e, jnp.concatenate([v, ones], 1)))
+        for s, e, pair in zip(chosen, es_now, both):
             es[w, s] = e
-            both = dot(e, jnp.concatenate([v, ones], 1))
-            inv = 1.0 / both[:, 128:]
-            rd[w, :, s * 128 : (s + 1) * 128] = inv
-            mix[w, :, s * 128 : (s + 1) * 128] = (both[:, :128] * inv).astype(BF)
+            inv = 1.0 / pair[:, 128:]
+            rd[w, :, lanes_at(s * 128, 128)] = inv
+            mix[w, :, lanes_at(s * 128, 128)] = (pair[:, :128] * inv).astype(BF)
         return carry
 
     lax.fori_loop(low, high, attend, 0)
 
 
-def forward_out(take, wo, mix, put, work):
-    work[...] = dot(mix[...].reshape(512, 512), wo[...]).reshape(4, 128, 512)
+def forward_out(take, wo, mix, put, work, low, high):
+    count = high - low
+    got = dot(mix[low:high].reshape(count * 128, 512), wo[...])
+    work[low:high] = got.reshape(count, 128, 512)
 
     def project(w, carry):
         put(w, take(w).astype(F32) + work[w])
         return carry
 
-    lax.fori_loop(0, 4, project, 0)
+    lax.fori_loop(low, high, project, 0)
 
 
 def backward_do(take, wo, cw, do, low, high):
@@ -182,47 +197,61 @@
         do[low:high, :, cols] = got.reshape(count, 128, 256)
 
 
-def backward_out(mix, cw, g):
+def backward_out(mix, cw, put):
     for j in range(2):
         cols = slice(j * 256, (j + 1) * 256)
         got = dot(mix[:, :, cols].reshape(512, 256), cw[...].reshape(512, 512), TN).astype(BF)
-        g[j, 1, 1, 0:2] = got[:, 0:256].reshape(2, 4, 2, 16, 256)
-        g[j, 1, 1, 2:4] = got[:, 256:512].reshape(2, 4, 2, 16, 256)
-
-
-def backward_attend(pr, es, rd, mix, do, dpr, low, high):
+        put(3, j, jnp.concatenate([got[:, 0:256], got[:, 256:512]], 0))
+
+
+def backward_values(es, rd, do, ge, dpr, low, high):
+    masks = head_masks()
+
+    def attend(w, carry):
+        sets = [slice(s * 128, (s + 1) * 128) for s in range(4)]
+        g1 = [(do[w, :, lanes] * rd[w, :, lanes]).astype(BF) for lanes in sets]
+        tall = [dot(es[w, s], g1[s], TN) for s in range(4)]
+        for s in range(4):
+            ge[w, :, sets[s]] = g1[s]
+            dv = merge_heads(tall[s], masks)
+            dpr[w, :, 1024 + s * 128 : 1024 + (s + 1) * 128] = dv.astype(BF)
+        return carry
+
+    lax.fori_loop(low, high, attend, 0)
+
+
+def backward_scores(pr, es, mix, ge, dpr, low, high):
     masks = head_masks()
     ones = spread_heads(jnp.ones((128, 128), BF), masks)
 
     def attend(w, carry):
+        sets = [slice(s * 128, (s + 1) * 128) for s in range(4)]
+        t = []
         for s in range(4):
-            lanes = slice(s * 128, (s + 1) * 128)
-            q = pr[w, :, lanes]
+            v = spread_heads(pr[w, :, 1024 + s * 128 : 1024 + (s + 1) * 128], masks)
+            g1 = ge[w, :, sets[s]]
+            g2 = (-(g1.astype(F32) * mix[w, :, sets[s]].astype(F32))).astype(BF)
+            t.append(dot(jnp.concatenate([g1, g2], 1), jnp.concatenate([v, ones], 1), NT))
+        ds = [(es[w, s].astype(F32) * t[s]).astype(BF) for s in range(4)]
+        dq, dk = [], []
+        for s in range(4):
             k = spread_heads(pr[w, :, 512 + s * 128 : 512 + (s + 1) * 128], masks)
-            v = spread_heads(pr[w, :, 1024 + s * 128 : 1024 + (s + 1) * 128], masks)
-            e = es[w, s]
-            g1 = do[w, :, lanes] * rd[w, :, lanes]
-            g2 = g1 * mix[w, :, lanes].astype(F32)
-            g1 = g1.astype(BF)
-            t = dot(jnp.concatenate([g1, (-g2).astype(BF)], 1), jnp.concatenate([v, ones], 1), NT)
-            ds = (e.astype(F32) * t).astype(BF)
-            dq = dot(ds, k) * SCALE
-            dk = merge_heads(dot(ds, q, TN), masks) * SCALE
-            dv = merge_heads(dot(e, g1, TN), masks)
-            dpr[w, :, lanes] = dq.astype(BF)
-            dpr[w, :, 512 + s * 128 : 512 + (s + 1) * 128] = dk.astype(BF)
-            dpr[w, :, 1024 + s * 128 : 1024 + (s + 1) * 128] = dv.astype(BF)
+            dq.append(dot(ds[s], k) * SCALE)
+            dk.append(merge_heads(dot(ds[s], pr[w, :, sets[s]], TN), masks) * SCALE)
+        for s in range(4):
+            dpr[w, :, sets[s]] = dq[s].astype(BF)
+            dpr[w, :, 512 + s * 128 : 512 + (s + 1) * 128] = dk[s].astype(BF)
         return carry
 
     lax.fori_loop(low, high, attend, 0)
 
 
-def backward_weights(n, dpr, g):
-    for c in range(3):
+def backward_weights(n, dpr, put, kinds):
+    for c in kinds:
         for j in range(2):
             cols = slice(c * 512 + j * 256, c * 512 + (j + 1) * 256)
             got = dot(n[...].reshape(512, 512), dpr[:, :, cols].reshape(512, 256), TN)
-            g[j, c // 2, c % 2] = got.astype(BF).reshape(4, 4, 2, 16, 256)
+            put(c, j, got.astype(BF))
 
 
 def backward_tokens(take, wq, cw, dpr, put, work, low, high):
@@ -371,30 +400,31 @@
     return (row_lat, lon, row_mp), (lat, col, mp), (row_lat, col, row_mp)
 
 
-SENDS = 112
+SENDS = 176
 
 
 def pair_kernel(
     fc, cc, wqp, wop, wqs, wos,
-    ro, gfo, f_plain, f_shift,
+    ro, gfo, f_early, f_late, f_shift,
     x, hx, cx, rs, rp, gs, gp, gf, rn,
     fqp, fop, fqs, fos,
     n_p, pr_p, es_p, rd_p, mix_p,
     n_s, pr_s, es_s, rd_s, mix_s,
-    cw, do, dpr, cn,
-    g_plain, g_shift,
+    cw, do, dpr, ge, cn,
+    g_early, g_late, g_shift,
     *rest,
 ):
-    sums, (send, recv, local) = rest[:14], rest[14:]
+    sums, (send, recv, local) = rest[:21], rest[21:]
     lat, lon, mp = place()
     row_prev, col_prev, corner_prev = around(lat, lon, mp, -1)
     row_next, col_next, corner_next = around(lat, lon, mp, 1)
     go = Sender(send, recv)
-    sum_plain = Sum(go, g_plain, f_plain, *sums[:7])
-    sum_shift = Sum(go, g_shift, f_shift, *sums[7:])
-    near, far, sibling, core = sum_plain.near, sum_plain.far, sum_plain.sibling, sum_plain.core
+    early = Sum(go, g_early, f_early, *sums[:7])
+    late = Sum(go, g_late, f_late, *sums[7:14])
+    shifted = Sum(go, g_shift, f_shift, *sums[14:])
+    near, far, sibling, core = early.near, early.far, early.sibling, early.core
     barrier(
-        sum_plain.peers
+        early.peers
         + [row_prev, col_prev, corner_prev, row_next, col_next, corner_next]
     )
     lanes = pl.ds(pl.multiple_of(mp * 256, 256), 256)
@@ -421,7 +451,7 @@
         return go(src.at[rows], dst.at[there], peer), dst.at[here]
 
     y, z = lax.rem(lat, 4), lon // 2
-    along_y, along_z = sum_plain.ways[0][1], sum_plain.ways[0][3]
+    along_y, along_z = early.ways[0][1], early.ways[0][3]
     rows_s = pl.ds(pl.multiple_of(core * 256 + y * 64, 64), 64)
     half_s = pl.ds(pl.multiple_of(core * 256, 256), 256)
     at_o = core * 128 + z * 32
@@ -467,14 +497,13 @@
     forward_norm(take_x, n_p, 0, 4)
     for copy in others:
         copy.wait()
-    passed = pass_on(qkv_p[0])
-    for c in range(3):
-        passed_next = pass_on(qkv_p[c + 1]) if c < 2 else None
-        passed.wait_recv()
-        if c == 2:
-            out_p = weight_out(wop, fop, far)
-        forward_project(n_p, fqp, pr_p, 0, 4, (c,))
-        passed = passed_next
+    forward_project(n_p, fqp, pr_p, 0, 4, (mp,))
+    passed = [pass_on(part) for part in qkv_p]
+    out_p = weight_out(wop, fop, far)
+    forward_attend(pr_p, es_p, rd_p, mix_p, None, 0, 4, (mp * 2, mp * 2 + 1))
+    for copy in passed:
+        copy.wait_recv()
+    forward_project(n_p, fqp, pr_p, 0, 4, (1 - mp,))
     for copy in over_x:
         copy.wait_recv()
     unsent.extend(over_x)
@@ -485,15 +514,18 @@
         spot = fos.at[here_o]
         spread.append(go(spot, spot, along_z(step)))
     cot_copy = go(cc.at[other_rows], cn.at[:, :, lanes], near)
-    forward_attend(pr_p, es_p, rd_p, mix_p, None, 0, 4)
+    others_sets = (2 - mp * 2, 3 - mp * 2)
+    forward_attend(pr_p, es_p, rd_p, mix_p, None, 0, 3, others_sets)
     pass_on(out_p).wait_recv()
-    forward_out(take_x, fop, mix_p, put_hidden, do)
+    forward_out(take_x, fop, mix_p, put_hidden, do, 0, 3)
 
     halos = [
         go(hx.at[0, own], hx.at[4, own], row_prev),
         go(hx.at[own, 0], hx.at[own, 4], col_prev),
         go(hx.at[0, 0], hx.at[4, 4], corner_prev),
     ]
+    forward_attend(pr_p, es_p, rd_p, mix_p, None, 3, 4, others_sets)
+    forward_out(take_x, fop, mix_p, put_hidden, do, 3, 4)
 
     def take_hidden(w):
         return window(hx, w, 1)
@@ -532,7 +564,7 @@
     def put_result(w, value):
         put_window(rs, w, value.astype(BF))
 
-    forward_out(take_hidden, fos, mix_s, put_result, do)
+    forward_out(take_hidden, fos, mix_s, put_result, do, 0, 4)
 
     low, high = pl.ds(0, 3), pl.ds(1, 3)
 
@@ -541,10 +573,10 @@
             go(src.at[3, low], dst.at[0, high], row_next),
             go(src.at[low, 3], dst.at[high, 0], col_next),
             go(src.at[3, 3], dst.at[0, 0], corner_next),
-            keep(src.at[low, low], dst.at[high, high]),
         ]
 
     result_halos = narrow(rs, rp)
+    result_halos.append(keep(rs.at[low, low], rp.at[high, high]))
 
     def take_cot(w):
         return window(cx, w, 1)
@@ -552,15 +584,22 @@
     def put_grad(w, value):
         put_window(gs, w, value.astype(BF))
 
+    def put_shift(kind, j, value):
+        g_shift[j, kind // 2, kind % 2] = value.reshape(4, 4, 2, 16, 256)
+
     for copy in cot_halos:
         copy.wait()
-    backward_do(take_cot, fos, cw, do, 0, 4)
-    backward_out(mix_s, cw, g_shift)
-    backward_attend(pr_s, es_s, rd_s, mix_s, do, dpr, 0, 4)
-    backward_tokens(take_hidden, fqs, cw, dpr, put_grad, do, 0, 4)
-    grad_halos = narrow(gs, gp)
-    backward_weights(n_s, dpr, g_shift)
-    sum_shift.step0()
+    for first, end in ((1, 4), (0, 1)):
+        backward_do(take_cot, fos, cw, do, first, end)
+        backward_values(es_s, rd_s, do, ge, dpr, first, end)
+        backward_scores(pr_s, es_s, mix_s, ge, dpr, first, end)
+        backward_tokens(take_hidden, fqs, cw, dpr, put_grad, do, first, end)
+        if first == 1:
+            grad_halos = narrow(gs, gp)
+    grad_kept = keep(gs.at[low, low], gp.at[high, high])
+    backward_out(mix_s, cw, put_shift)
+    backward_weights(n_s, dpr, put_shift, (0, 1, 2))
+    shifted.step0()
     for copy in result_halos:
         copy.wait()
 
@@ -578,18 +617,28 @@
     def put_fields(w, value):
         put_rows(gf, w, value.astype(BF))
 
-    grad_halos.pop().wait()
+    def put_plain(kind, j, value):
+        to = g_early if kind >= 2 else g_late
+        for part in range(2):
+            half = value[:, part * 128 : (part + 1) * 128]
+            to[j, kind % 2, part] = half.reshape(4, 4, 2, 16, 128)
+
+    grad_kept.wait()
     backward_do(take_back, fop, cw, do, 3, 4)
-    backward_attend(pr_p, es_p, rd_p, mix_p, do, dpr, 3, 4)
+    backward_values(es_p, rd_p, do, ge, dpr, 3, 4)
+    backward_scores(pr_p, es_p, mix_p, ge, dpr, 3, 4)
     for copy in grad_halos:
         copy.wait()
+    shifted.step1()
     backward_do(take_back, fop, cw, do, 0, 3)
-    backward_out(mix_p, cw, g_plain)
-    sum_shift.step1()
-    backward_attend(pr_p, es_p, rd_p, mix_p, do, dpr, 0, 3)
-    sum_shift.step2()
-    backward_weights(n_p, dpr, g_plain)
-    sum_plain.step0()
+    backward_values(es_p, rd_p, do, ge, dpr, 0, 3)
+    backward_weights(n_p, dpr, put_plain, (2,))
+    backward_out(mix_p, cw, put_plain)
+    early.step0()
+    backward_scores(pr_p, es_p, mix_p, ge, dpr, 0, 3)
+    early.step1()
+    backward_weights(n_p, dpr, put_plain, (0, 1))
+    late.step0()
     for half in range(2):
         backward_tokens(take_x, fqp, cw, dpr, put_fields, do, half * 2, half * 2 + 2)
         rows = pl.ds(half * 8, 8)
@@ -597,18 +646,25 @@
         ends.append(go(gf.at[rows, :, away], gfo.at[there], near))
         ends.append(keep(gf.at[rows, :, lanes], gfo.at[there]))
         if half == 0:
-            sum_plain.step1()
-            sum_shift.step3()
-    sum_shift.step4()
-    sum_plain.step2()
-    sum_shift.step5()
-    sum_plain.step3()
-    sum_shift.step6()
-    sum_plain.step4()
-    sum_plain.step5()
-    sum_plain.step6()
-    sum_shift.last()
-    sum_plain.last()
+            late.step1()
+            shifted.step2()
+    early.step2()
+    shifted.step3()
+    late.step2()
+    early.step3()
+    shifted.step4()
+    late.step3()
+    early.step4()
+    shifted.step5()
+    late.step4()
+    early.step5()
+    shifted.step6()
+    late.step5()
+    early.step6()
+    late.step6()
+    shifted.last()
+    early.last()
+    late.last()
     for copy in ends:
         copy.wait()
     for copy in unsent:
@@ -616,7 +672,9 @@
 
 
 def last_kernel(
-    factor, f_plain, f_shift, r, gf, qkv_p, out_p, qkv_s, out_s, ro, gfo, raw, wide, held, came, gone
+    factor, f_early, f_late, f_shift, r, gf,
+    qkv_p, out_p, qkv_s, out_s, ro, gfo,
+    raw, wide, held, came, gone,
 ):
     coming, going = [], []
 
@@ -625,23 +683,31 @@
         copy.start()
         to.append(copy)
 
+    for n in range(4):
+        move(f_shift.at[pl.ds(n * 512, 512)], raw.at[n], came.at[n], coming)
+    for n, src in enumerate((r, gf)):
+        move(src, held.at[n], came.at[4 + n], coming)
+    for n in range(4):
+        for part in range(2):
+            src = (f_late, f_early)[n // 2].at[n % 2, part]
+            dst = raw.at[4 + n, :, pl.ds(part * 128, 128)]
+            move(src, dst, came.at[6 + n * 2 + part], coming)
     for n in range(8):
-        rows = pl.ds(n % 4 * 512, 512)
-        move((f_plain, f_shift)[n // 4].at[rows], raw.at[n], came.at[n], coming)
-    for n, src in enumerate((r, gf)):
-        move(src, held.at[n], came.at[8 + n], coming)
-    for n in range(8):
-        coming[n].wait()
+        if n < 4:
+            coming[n].wait()
+        else:
+            coming[n * 2 - 2].wait()
+            coming[n * 2 - 1].wait()
         wide[n] = raw[n].astype(F32) * factor
         if n % 4 < 3:
-            move(wide.at[n], (qkv_p, qkv_s)[n // 4].at[n % 4], gone.at[n], going)
+            move(wide.at[n], (qkv_s, qkv_p)[n // 4].at[n % 4], gone.at[n], going)
         else:
             for k in range(2):
                 cols = pl.ds(k * 256, 256)
-                dst = (out_p, out_s)[n // 4].at[:, cols]
+                dst = (out_s, out_p)[n // 4].at[:, cols]
                 move(wide.at[n, cols], dst, gone.at[8 + n // 4 * 2 + k], going)
     for n, dst in enumerate((ro, gfo)):
-        coming[8 + n].wait()
+        coming[4 + n].wait()
         move(held.at[n], dst, gone.at[12 + n], going)
     for copy in going:
         copy.wait()
@@ -662,22 +728,27 @@
     ((4, 128, 512), F32),
     ((4, 128, 512), BF),
 )
-SUM = (
-    (2, 2, 4, 4, 2, 16, 256),
-    (2, 2, 4, 4, 2, 16, 256),
-    (2, 3, 2, 4, 2, 16, 256),
-    (2, 2, 4, 2, 16, 256),
-    (2, 3, 2, 2, 16, 256),
-    (2, 2, 2, 16, 256),
-    (3, 2, 2, 16, 256),
-)
+
+
+def sum_shapes(width):
+    return [
+        (2, 2, 4, 4, 2, 16, width),
+        (2, 2, 4, 4, 2, 16, width),
+        (2, 3, 2, 4, 2, 16, width),
+        (2, 2, 4, 2, 16, width),
+        (2, 3, 2, 2, 16, width),
+        (2, 2, 2, 16, width),
+        (3, 2, 2, 16, width),
+    ]
+
+
 SCRATCH = (
     [(s, BF) for s in (ROWS, WIDE, WIDE, GRID, GRID, GRID, GRID, ROWS, ROWS)]
     + [((3, 512, 512), BF), ((512, 512), BF)] * 2
     + list(SAVED) * 2
-    + [((4, 128, 512), BF), ((4, 128, 512), F32), ((4, 128, 1536), BF), (ROWS, BF)]
-    + [((2, 2, 2, 4, 4, 2, 16, 256), BF)] * 2
-    + [(s, BF) for s in SUM] * 2
+    + [((4, 128, 512), BF), ((4, 128, 512), F32), ((4, 128, 1536), BF), ((4, 128, 512), BF), (ROWS, BF)]
+    + [((2, 2, 2, 4, 4, 2, 16, width), BF) for width in (128, 128, 256)]
+    + [(s, BF) for width in (128, 128, 256) for s in sum_shapes(width)]
 )
 
 
@@ -685,12 +756,12 @@
     factor = (fields.shape[0] * fields.shape[1] * 64) ** -0.5
     vmem = pl.BlockSpec(memory_space=pltpu.VMEM)
     hbm = pl.BlockSpec(memory_space=pl.ANY)
-    f_shape = (2, 2, 4, 4, 2, 16, 256)
-    result, grad_fields, f_plain, f_shift = pl.pallas_call(
+    f_half, f_whole = (2, 2, 4, 4, 2, 16, 128), (2, 2, 4, 4, 2, 16, 256)
+    result, grad_fields, f_early, f_late, f_shift = pl.pallas_call(
         pair_kernel,
-        out_shape=[shape(*HELD), shape(*HELD), shape(*f_shape), shape(*f_shape)],
+        out_shape=[shape(*HELD), shape(*HELD), shape(*f_half), shape(*f_half), shape(*f_whole)],
         in_specs=[hbm] * 6,
-        out_specs=[vmem] * 4,
+        out_specs=[vmem] * 5,
         scratch_shapes=[pltpu.VMEM(s, t) for s, t in SCRATCH]
         + [
             pltpu.SemaphoreType.DMA((SENDS,)),
@@ -712,17 +783,23 @@
     qkv_p, out_p, qkv_s, out_s, result, grad_fields = pl.pallas_call(
         functools.partial(last_kernel, factor),
         out_shape=[qkv, out, qkv, out, shape(*HELD), shape(*HELD)],
-        in_specs=[hbm] * 4,
+        in_specs=[hbm] * 5,
         out_specs=[hbm] * 6,
         scratch_shapes=[
             pltpu.VMEM((8, 512, 256), BF),
             pltpu.VMEM((8, 512, 256), F32),
             pltpu.VMEM((2,) + HELD, BF),
-            pltpu.SemaphoreType.DMA((10,)),
+            pltpu.SemaphoreType.DMA((14,)),
             pltpu.SemaphoreType.DMA((14,)),
         ],
         compiler_params=pltpu.CompilerParams(vmem_limit_bytes=VMEM_LIMIT),
-    )(f_plain.reshape(2048, 256), f_shift.reshape(2048, 256), result, grad_fields)
+    )(
+        f_early.reshape(2, 2, 512, 128),
+        f_late.reshape(2, 2, 512, 128),
+        f_shift.reshape(2048, 256),
+        result,
+        grad_fields,
+    )
     return (
         result,
         grad_fields,

time: 103 us -> 94.1 us (0.914)
  Pallas kernels: 102 us -> 93.2 us
    pallas_call x1, Pallas kernels: 98.9 us -> 89.6 us  [on_device(): pl.pallas_call(pair_kernel, out_shape=[shape(*HELD), shape(*HELD), shape(...]
where the time goes in v4:
time: 94.1 us; the launch traced here: 94 us
  Pallas kernels  93.2 us (99%)
    pallas_call x1, Pallas kernels, on_device(): pl.pallas_call(pair_kernel, out_shape=[shape(*HELD), shape(*HELD), shape(...  89.6 us
    pallas_call x1, Pallas kernels, on_device(): pl.pallas_call(functools.partial(last_kernel, factor), out_shape=[qkv, ou...  3.56 us

profile of v4, /device:TPU:1, one launch (start us, length us, event | category | flops | bytes accessed | tf_op | source)
XLA Modules:
  0.0 94.0 jit_solution(4935452756225540646)
XLA Ops:
  0.6 89.6 %shard_map.109 = (bf16[32,32,256]{2,1,0:T(8,128)(2,1)}, bf16[32,32,256]{2,1,0:T(8,128)(2,1)}, bf16[2,2,4,4,2,16,128]{6,5,4,3,2,1,0:T(8,128)(2,1)}, bf16[2,2,4,4,...) custom-call(bf16[32,32,256]{2,1,0:T(8,128)(2,1)} %fc.1, bf16[32,32,256]{2,1,0:T(8,128)(2,1)} %cc.1, ...), custom_call_target="tpu_custom_call" | custom-call | tf_op jit(solution)/shard_map/pallas_call | solution.py:760
  90.2 3.6 %shard_map.110 = (f32[3,512,256]{2,1,0:T(8,128)}, f32[256,512]{1,0:T(8,128)}, f32[3,512,256]{2,1,0:T(8,128)}, f32[256,512]{1,0:T(8,128)}, bf16[32,32,256]{2,1,0:T(8,128)(2,1)}, /*index=5*/bf16[32,32,256]{2,1,0:T(8,128)(2,1)}) custom-call(bf16[2,2,512,128]{3,2,1,0:T(8,128)(2,1)} %bitcast.10, bf16[2,2,512,128]{3,2,1,0:T(8,128)(2,1)} %bitcast.11, ...), custom_call_target="tpu_custom_call" | custom-call | tf_op jit(solution)/shard_map/pallas_call | solution.py:783

commit v5 on v4

--- a/solution.py
+++ b/solution.py
@@ -168,7 +168,7 @@
             mix[w, :, lanes_at(s * 128, 128)] = (pair[:, :128] * inv).astype(BF)
         return carry
 
-    lax.fori_loop(low, high, attend, 0)
+    lax.fori_loop(low, high, attend, 0, unroll=2 if (high - low) % 2 == 0 else 1)
 
 
 def forward_out(take, wo, mix, put, work, low, high):
@@ -217,7 +217,7 @@
             dpr[w, :, 1024 + s * 128 : 1024 + (s + 1) * 128] = dv.astype(BF)
         return carry
 
-    lax.fori_loop(low, high, attend, 0)
+    lax.fori_loop(low, high, attend, 0, unroll=2 if (high - low) % 2 == 0 else 1)
 
 
 def backward_scores(pr, es, mix, ge, dpr, low, high):
@@ -243,7 +243,7 @@
             dpr[w, :, 512 + s * 128 : 512 + (s + 1) * 128] = dk[s].astype(BF)
         return carry
 
-    lax.fori_loop(low, high, attend, 0)
+    lax.fori_loop(low, high, attend, 0, unroll=2 if (high - low) % 2 == 0 else 1)
 
 
 def backward_weights(n, dpr, put, kinds):
@@ -430,6 +430,7 @@
     lanes = pl.ds(pl.multiple_of(mp * 256, 256), 256)
     away = pl.ds(pl.multiple_of((1 - mp) * 256, 256), 256)
     other_rows = pl.ds((1 - mp) * 16, 16)
+    other_half = [pl.ds((1 - mp) * 16 + half * 8, 8) for half in range(2)]
     own_rows = pl.ds(mp * 16, 16)
     own = pl.ds(0, 4)
     kept = []
@@ -470,8 +471,16 @@
         unsent.append(passed)
         return passed
 
-    fields_copy = go(fc.at[other_rows], x.at[:, :, lanes], near)
+    fields_copy = [
+        go(fc.at[other_half[half]], x.at[pl.ds(half * 8, 8), :, lanes], near) for half in range(2)
+    ]
     qkv_p = [weight(wqp, fqp, c, far) for c in range(3)]
+    out_p = weight_out(wop, fop, far)
+    over_x = [
+        go(wqs.at[:, rows_s], fqs.at[:, rows_s, lanes], near),
+        go(wos.at[rows_o], fos.at[there_o], near),
+    ]
+    cot_copy = go(cc.at[other_rows], cn.at[:, :, lanes], near)
     x_kept = keep(fc.at[own_rows], x.at[:, :, lanes])
     mp_rows = pl.ds(pl.multiple_of(mp * 256, 256), 256)
     others = [
@@ -488,22 +497,15 @@
     def put_hidden(w, value):
         put_window(hx, w, cells_of(value).astype(BF))
 
-    fields_copy.wait()
     x_kept.wait()
-    over_x = [
-        go(wqs.at[:, rows_s], fqs.at[:, rows_s, lanes], near),
-        go(wos.at[rows_o], fos.at[there_o], near),
-    ]
-    forward_norm(take_x, n_p, 0, 4)
-    for copy in others:
-        copy.wait()
-    forward_project(n_p, fqp, pr_p, 0, 4, (mp,))
+    for half in range(2):
+        fields_copy[half].wait()
+        forward_norm(take_x, n_p, half * 2, half * 2 + 2)
+        if half == 0:
+            for copy in others:
+                copy.wait()
+        forward_project(n_p, fqp, pr_p, half * 2, half * 2 + 2, (mp,))
     passed = [pass_on(part) for part in qkv_p]
-    out_p = weight_out(wop, fop, far)
-    forward_attend(pr_p, es_p, rd_p, mix_p, None, 0, 4, (mp * 2, mp * 2 + 1))
-    for copy in passed:
-        copy.wait_recv()
-    forward_project(n_p, fqp, pr_p, 0, 4, (1 - mp,))
     for copy in over_x:
         copy.wait_recv()
     unsent.extend(over_x)
@@ -513,15 +515,18 @@
         spread.append(go(spot, spot, along_y(step)))
         spot = fos.at[here_o]
         spread.append(go(spot, spot, along_z(step)))
-    cot_copy = go(cc.at[other_rows], cn.at[:, :, lanes], near)
+    forward_attend(pr_p, es_p, rd_p, mix_p, None, 0, 4, (mp * 2, mp * 2 + 1))
+    for copy in passed:
+        copy.wait_recv()
+    forward_project(n_p, fqp, pr_p, 0, 4, (1 - mp,))
     others_sets = (2 - mp * 2, 3 - mp * 2)
     forward_attend(pr_p, es_p, rd_p, mix_p, None, 0, 3, others_sets)
     pass_on(out_p).wait_recv()
     forward_out(take_x, fop, mix_p, put_hidden, do, 0, 3)
 
     halos = [
+        go(hx.at[own, 0], hx.at[own, 4], col_prev),
         go(hx.at[0, own], hx.at[4, own], row_prev),
-        go(hx.at[own, 0], hx.at[own, 4], col_prev),
         go(hx.at[0, 0], hx.at[4, 4], corner_prev),
     ]
     forward_attend(pr_p, es_p, rd_p, mix_p, None, 3, 4, others_sets)
@@ -530,6 +535,18 @@
     def take_hidden(w):
         return window(hx, w, 1)
 
+    cot_copy.wait()
+
+    def into_cells(w, carry):
+        put_window(cx, w, cells_of(rows_window(cn, w).astype(F32)).astype(BF))
+        return carry
+
+    lax.fori_loop(0, 4, into_cells, 0)
+    cot_halos = [
+        go(cx.at[0, own], cx.at[4, own], row_prev),
+        go(cx.at[own, 0], cx.at[own, 4], col_prev),
+        go(cx.at[0, 0], cx.at[4, 4], corner_prev),
+    ]
     for copy in spread:
         copy.wait()
     spot = fqs.at[:, half_s, away]
@@ -542,23 +559,15 @@
     cut = (lat * 2 + mp) == 15
     forward_attend(pr_s, es_s, rd_s, mix_s, cut, 0, 1)
 
-    cot_copy.wait()
-
-    def into_cells(w, carry):
-        put_window(cx, w, cells_of(rows_window(cn, w).astype(F32)).astype(BF))
-        return carry
-
-    lax.fori_loop(0, 4, into_cells, 0)
-    for copy in halos:
+    halos[0].wait()
+    forward_norm(take_hidden, n_s, 1, 2)
+    forward_project(n_s, fqs, pr_s, 1, 2)
+    forward_attend(pr_s, es_s, rd_s, mix_s, cut, 1, 2)
+    for copy in halos[1:]:
         copy.wait()
-    cot_halos = [
-        go(cx.at[0, own], cx.at[4, own], row_prev),
-        go(cx.at[own, 0], cx.at[own, 4], col_prev),
-        go(cx.at[0, 0], cx.at[4, 4], corner_prev),
-    ]
-    forward_norm(take_hidden, n_s, 1, 4)
-    forward_project(n_s, fqs, pr_s, 1, 4)
-    forward_attend(pr_s, es_s, rd_s, mix_s, cut, 1, 4)
+    forward_norm(take_hidden, n_s, 2, 4)
+    forward_project(n_s, fqs, pr_s, 2, 4)
+    forward_attend(pr_s, es_s, rd_s, mix_s, cut, 2, 4)
     passed_out.wait()
 
     def put_result(w, value):
@@ -627,9 +636,9 @@
     backward_do(take_back, fop, cw, do, 3, 4)
     backward_values(es_p, rd_p, do, ge, dpr, 3, 4)
     backward_scores(pr_p, es_p, mix_p, ge, dpr, 3, 4)
+    shifted.step1()
     for copy in grad_halos:
         copy.wait()
-    shifted.step1()
     backward_do(take_back, fop, cw, do, 0, 3)
     backward_values(es_p, rd_p, do, ge, dpr, 0, 3)
     backward_weights(n_p, dpr, put_plain, (2,))

time: 94.1 us -> 90.2 us (0.959)
  Pallas kernels: 93.2 us -> 89.3 us
    pallas_call x1, Pallas kernels: 89.6 us -> 85.7 us  [on_device(): pl.pallas_call(pair_kernel, out_shape=[shape(*HELD), shape(*HELD), shape(...]
where the time goes in v5:
time: 90.2 us; the launch traced here: 90.1 us
  Pallas kernels  89.3 us (99%)
    pallas_call x1, Pallas kernels, on_device(): pl.pallas_call(pair_kernel, out_shape=[shape(*HELD), shape(*HELD), shape(...  85.7 us
    pallas_call x1, Pallas kernels, on_device(): pl.pallas_call(functools.partial(last_kernel, factor), out_shape=[qkv, ou...  3.56 us

profile of v5, /device:TPU:1, one launch (start us, length us, event | category | flops | bytes accessed | tf_op | source)
XLA Modules:
  0.0 90.1 jit_solution(11640808888071926346)
XLA Ops:
  0.6 85.7 %shard_map.109 = (bf16[32,32,256]{2,1,0:T(8,128)(2,1)}, bf16[32,32,256]{2,1,0:T(8,128)(2,1)}, bf16[2,2,4,4,2,16,128]{6,5,4,3,2,1,0:T(8,128)(2,1)}, bf16[2,2,4,4,...) custom-call(bf16[32,32,256]{2,1,0:T(8,128)(2,1)} %fc.1, bf16[32,32,256]{2,1,0:T(8,128)(2,1)} %cc.1, ...), custom_call_target="tpu_custom_call" | custom-call | tf_op jit(solution)/shard_map/pallas_call | solution.py:769
  86.3 3.6 %shard_map.110 = (f32[3,512,256]{2,1,0:T(8,128)}, f32[256,512]{1,0:T(8,128)}, f32[3,512,256]{2,1,0:T(8,128)}, f32[256,512]{1,0:T(8,128)}, bf16[32,32,256]{2,1,0:T(8,128)(2,1)}, /*index=5*/bf16[32,32,256]{2,1,0:T(8,128)(2,1)}) custom-call(bf16[2,2,512,128]{3,2,1,0:T(8,128)(2,1)} %bitcast.10, bf16[2,2,512,128]{3,2,1,0:T(8,128)(2,1)} %bitcast.11, ...), custom_call_target="tpu_custom_call" | custom-call | tf_op jit(solution)/shard_map/pallas_call | solution.py:792

commit v6 on v5

--- a/solution.py
+++ b/solution.py
@@ -405,8 +405,8 @@
 
 def pair_kernel(
     fc, cc, wqp, wop, wqs, wos,
-    ro, gfo, f_early, f_late, f_shift,
-    x, hx, cx, rs, rp, gs, gp, gf, rn,
+    ro, gfo, f_early_out, f_late_out, f_shift_out,
+    f_early, f_late, f_shift, x, hx, cx, rs, rp, gs, gp, gf, rn,
     fqp, fop, fqs, fos,
     n_p, pr_p, es_p, rd_p, mix_p,
     n_s, pr_s, es_s, rd_s, mix_s,
@@ -669,11 +669,14 @@
     early.step5()
     shifted.step6()
     late.step5()
+    shifted.last()
+    ends.append(keep(f_shift, f_shift_out))
     early.step6()
     late.step6()
-    shifted.last()
     early.last()
+    ends.append(keep(f_early, f_early_out))
     late.last()
+    ends.append(keep(f_late, f_late_out))
     for copy in ends:
         copy.wait()
     for copy in unsent:
@@ -763,19 +766,19 @@
 
 def on_device(fields, qkv_plain, out_plain, qkv_shift, out_shift, cotangent):
     factor = (fields.shape[0] * fields.shape[1] * 64) ** -0.5
-    vmem = pl.BlockSpec(memory_space=pltpu.VMEM)
     hbm = pl.BlockSpec(memory_space=pl.ANY)
     f_half, f_whole = (2, 2, 4, 4, 2, 16, 128), (2, 2, 4, 4, 2, 16, 256)
     result, grad_fields, f_early, f_late, f_shift = pl.pallas_call(
         pair_kernel,
         out_shape=[shape(*HELD), shape(*HELD), shape(*f_half), shape(*f_half), shape(*f_whole)],
         in_specs=[hbm] * 6,
-        out_specs=[vmem] * 5,
-        scratch_shapes=[pltpu.VMEM(s, t) for s, t in SCRATCH]
+        out_specs=[hbm] * 5,
+        scratch_shapes=[pltpu.VMEM(s, BF) for s in (f_half, f_half, f_whole)]
+        + [pltpu.VMEM(s, t) for s, t in SCRATCH]
         + [
             pltpu.SemaphoreType.DMA((SENDS,)),
             pltpu.SemaphoreType.DMA((SENDS,)),
-            pltpu.SemaphoreType.DMA((12,)),
+            pltpu.SemaphoreType.DMA((15,)),
         ],
         compiler_params=pltpu.CompilerParams(
             collective_id=0, has_side_effects=True, vmem_limit_bytes=VMEM_LIMIT

time: 90.2 us -> 89.1 us (0.988)
  Pallas kernels: 89.3 us -> 88.1 us
    pallas_call x1, Pallas kernels: 85.7 us -> 84.6 us  [on_device(): pl.pallas_call(pair_kernel, out_shape=[shape(*HELD), shape(*HELD), shape(...]
where the time goes in v6:
time: 89.1 us; the launch traced here: 88.9 us
  Pallas kernels  88.1 us (99%)
    pallas_call x1, Pallas kernels, on_device(): pl.pallas_call(pair_kernel, out_shape=[shape(*HELD), shape(*HELD), shape(...  84.6 us
    pallas_call x1, Pallas kernels, on_device(): pl.pallas_call(functools.partial(last_kernel, factor), out_shape=[qkv, ou...  3.56 us

profile of v6, /device:TPU:1, one launch (start us, length us, event | category | flops | bytes accessed | tf_op | source)
XLA Modules:
  0.0 88.9 jit_solution(11974822244375462963)
XLA Ops:
  0.6 84.6 %shard_map.109 = (bf16[32,32,256]{2,1,0:T(8,128)(2,1)}, bf16[32,32,256]{2,1,0:T(8,128)(2,1)}, bf16[2,2,4,4,2,16,128]{6,5,4,3,2,1,0:T(8,128)(2,1)}, bf16[2,2,4,4,...) custom-call(bf16[32,32,256]{2,1,0:T(8,128)(2,1)} %fc.1, bf16[32,32,256]{2,1,0:T(8,128)(2,1)} %cc.1, ...), custom_call_target="tpu_custom_call" | custom-call | tf_op jit(solution)/shard_map/pallas_call | solution.py:771
  85.2 3.6 %shard_map.110 = (f32[3,512,256]{2,1,0:T(8,128)}, f32[256,512]{1,0:T(8,128)}, f32[3,512,256]{2,1,0:T(8,128)}, f32[256,512]{1,0:T(8,128)}, bf16[32,32,256]{2,1,0:T(8,128)(2,1)}, /*index=5*/bf16[32,32,256]{2,1,0:T(8,128)(2,1)}) custom-call(bf16[2,2,512,128]{3,2,1,0:T(8,128)(2,1)} %bitcast.10, bf16[2,2,512,128]{3,2,1,0:T(8,128)(2,1)} %bitcast.11, ...), custom_call_target="tpu_custom_call" | custom-call | tf_op jit(solution)/shard_map/pallas_call | solution.py:795
